TPU v7x, 256 devices: a whole 4x4x8 slice. The times are simulated.
256 devices in a mesh: row: 64 (over x_hi, y, z), col: 4 (over x_lo, core).
Axes of the slice: x: 4 (x_hi: 2, x_lo: 2; x = x_hi * 2 + x_lo), y: 4, z: 8, core: 2. Of those that a mesh axis runs over, the one named last changes fastest.
Arguments:
- weights: bfloat16 [3, 8192, 28672], P(None, 'row', 'col'), may hold values from -6 to 6
- left_outer: bfloat16 [64, 64], replicated, may hold values from -0.75 to 0.75
- left_inner: bfloat16 [128, 128], replicated, may hold values from -0.5 to 0.5
- right_outer: bfloat16 [224, 224], replicated, may hold values from -0.375 to 0.375
- right_inner: bfloat16 [128, 128], replicated, may hold values from -0.5 to 0.5
Outputs:
- rotated: bfloat16 [3, 128, 64, 28672], P(None, 'row', None, 'col')
- scales: float32 [3, 128, 64, 224], P(None, 'row', None, 'col')
All inputs are finite; a program needn't handle non-finite values.
Results may differ from a plain program's by a relative error of at most 0.0064.
Values may be sent and summed in bfloat16 or wider, within the bound.
No kernel may reach another device: no remote copies, remote signals or barrier semaphores. Data moves between devices by JAX's collectives and lax.ppermute only.
A program may use at most 128 MiB of HBM per device.

v0:
```python
import functools

import jax
import jax.numpy as jnp
import numpy as np
from jax import lax
from jax.experimental import pallas as pl
from jax.experimental.pallas import tpu as pltpu
from jax.sharding import Mesh
from jax.sharding import PartitionSpec as P

BF16 = jnp.bfloat16
F32 = jnp.float32
XH, Y, Z, XL, CORE = "xh", "y", "z", "xl", "core"
AXES = (XH, Y, Z, XL, CORE)
SIZES = (2, 4, 8, 2, 2)
WIDTH = 7168
BLOCKS = 56
VMEM = 24 * 1024 * 1024
INNER_VMEM = 60 * 1024 * 1024
WHOLE = pl.BlockSpec(memory_space=pltpu.VMEM)
ORDER = pl.BlockSpec(memory_space=pl.ANY)


def matmul(left, right):
    return jnp.dot(left, right, preferred_element_type=F32)


def blocks_of(count):
    return jax.ShapeDtypeStruct((count, BLOCKS, 128), BF16)


def cost(flops, passes):
    return pl.CostEstimate(
        flops=flops, bytes_accessed=passes * 128 * WIDTH * 2, transcendentals=0
    )


def inner_kernel(matrix, outs, xl_ref, w_ref, li_ref, ri_ref, *refs):
    o_refs, (held, turned, packed, sems, out_sems) = refs[-5 - outs : -5], refs[-5:]
    tiles = 4
    tile = WIDTH // tiles
    copies = [
        pltpu.make_async_copy(
            w_ref.at[matrix, :, pl.ds(t * tile, tile)], held.at[t], sems.at[t]
        )
        for t in range(tiles)
    ]
    for copy in copies:
        copy.start()
    ri = ri_ref[...]
    zero = jnp.zeros_like(ri)
    pair = jnp.concatenate(
        [
            jnp.concatenate([ri, zero], axis=1),
            jnp.concatenate([zero, ri], axis=1),
        ],
        axis=0,
    )
    li = li_ref[...]
    for t in range(tiles):
        copies[t].wait()
        pairs = tile // 256
        stacked = jnp.concatenate(
            [held[t, :, c * 256 : (c + 1) * 256] for c in range(pairs)], axis=0
        )
        first = lax.dot_general(
            stacked, pair, (((1,), (1,)), ((), ())), preferred_element_type=F32
        ).astype(BF16)
        first = jnp.concatenate(
            [first[c * 128 : (c + 1) * 128] for c in range(pairs)], axis=1
        )
        second = matmul(li, first)
        for p in range(tile // 128):
            turned[pl.ds(t * (tile // 128) + p, 128, stride=BLOCKS), :] = second[
                :, p * 128 : (p + 1) * 128
            ]
    parts = []
    for part in range(4):
        half = 1 - part // 2
        for r in range(32):
            if outs == 1:
                to = part * 32 + r
                row = to * BLOCKS
            else:
                at = part % 2 * 32 + r
                to = half * 64 + at
                row = pl.multiple_of((2 * at + (xl_ref[0] ^ half)) * BLOCKS, 8)
            packed[to] = turned[pl.ds(row, BLOCKS), :].astype(BF16)
        if outs == 1:
            here, there = part * 32, o_refs[0].at[pl.ds(part * 32, 32)]
        else:
            at = part % 2 * 32
            here, there = half * 64 + at, o_refs[half].at[pl.ds(at, 32)]
        parts.append(
            pltpu.make_async_copy(packed.at[pl.ds(here, 32)], there, out_sems.at[part])
        )
        parts[-1].start()
    for copy in parts:
        copy.wait()


def inner(weights, matrix, xl, li, ri, cuts, after=()):
    hbm = pl.BlockSpec(memory_space=pltpu.HBM)
    return pl.pallas_call(
        functools.partial(inner_kernel, matrix, cuts),
        in_specs=[pl.BlockSpec(memory_space=pltpu.SMEM), hbm, WHOLE, WHOLE]
        + [ORDER] * len(after),
        out_specs=[hbm] * cuts,
        out_shape=[blocks_of(128 // cuts)] * cuts,
        scratch_shapes=[
            pltpu.VMEM((4, 128, WIDTH // 4), BF16),
            pltpu.VMEM((128 * BLOCKS, 128), F32),
            pltpu.VMEM((128, BLOCKS, 128), BF16),
            pltpu.SemaphoreType.DMA((4,)),
            pltpu.SemaphoreType.DMA((4,)),
        ],
        compiler_params=pltpu.CompilerParams(vmem_limit_bytes=INNER_VMEM),
        cost_estimate=cost(4 * 128 * 128 * WIDTH, 2),
        name=f"inner{matrix}",
    )(xl, weights, li, ri, *after)


def mix_blocks(refs, rows, ro):
    columns = jnp.concatenate(
        [
            jnp.concatenate([ref[at].astype(F32) for ref, at in zip(refs, where)], axis=0)
            for where in rows
        ],
        axis=1,
    )
    return matmul(ro, columns.astype(BF16))


def right_kernel(ro_ref, *refs):
    sources, (o_ref, packed, sems) = refs[:4], refs[-3:]
    ro = ro_ref[...]
    parts = []
    for first in range(0, 64, 4):
        rows = range(first, first + 4)
        mixed = mix_blocks(sources, [(r,) * 4 for r in rows], ro)
        for at, r in enumerate(rows):
            lanes = slice(at * 128, at * 128 + 128)
            packed[2 * r] = mixed[:BLOCKS, lanes].astype(BF16)
            packed[2 * r + 1] = mixed[BLOCKS:, lanes].astype(BF16)
        if first % 16 == 12:
            done = pl.ds(2 * (first - 12), 32)
            parts.append(
                pltpu.make_async_copy(
                    packed.at[done], o_ref.at[done], sems.at[first // 16]
                )
            )
            parts[-1].start()
    for copy in parts:
        copy.wait()


def right(sources, ro, after=()):
    return pl.pallas_call(
        right_kernel,
        in_specs=[WHOLE] * 5 + [ORDER] * len(after),
        out_specs=pl.BlockSpec(memory_space=pltpu.HBM),
        out_shape=blocks_of(128),
        scratch_shapes=[
            pltpu.VMEM((128, BLOCKS, 128), BF16),
            pltpu.SemaphoreType.DMA((4,)),
        ],
        compiler_params=pltpu.CompilerParams(vmem_limit_bytes=VMEM),
        cost_estimate=cost(1153 * 10**6 * 20, 3),
        name="right",
    )(ro, *sources, *after)


def both_kernel(ro_ref, lo_ref, own_ref, other_ref, *refs):
    o_refs, turned = refs[-3:-1], refs[-1]
    ro = ro_ref[...]
    sources = (own_ref, own_ref, other_ref, other_ref)
    stride = 72
    for first in range(0, 64, 4):
        rows = range(first, first + 4)
        mixed = mix_blocks(sources, [(2 * r, 2 * r + 1) * 2 for r in rows], ro)
        for at, r in enumerate(rows):
            turned[pl.ds(r, 2 * BLOCKS, stride=stride), :] = mixed[
                :, at * 128 : at * 128 + 128
            ]
    lo = lo_ref[...]
    for half, ref in enumerate(o_refs):
        for first in range(0, BLOCKS, 14):
            x = jnp.concatenate(
                [
                    turned[
                        (half * BLOCKS + p) * stride : (half * BLOCKS + p) * stride + 64, :
                    ].astype(BF16)
                    for p in range(first, first + 14)
                ],
                axis=1,
            )
            ref[:, first * 128 : (first + 14) * 128] = matmul(lo, x).astype(BF16)


def both(own, other, ro, lo, after=()):
    return pl.pallas_call(
        both_kernel,
        in_specs=[WHOLE] * 4 + [ORDER] * len(after),
        out_specs=[WHOLE] * 2,
        out_shape=[jax.ShapeDtypeStruct((64, WIDTH), BF16)] * 2,
        scratch_shapes=[pltpu.VMEM((2 * BLOCKS * 72, 128), F32)],
        compiler_params=pltpu.CompilerParams(vmem_limit_bytes=VMEM),
        cost_estimate=cost(10 * 64 * BLOCKS * WIDTH, 3),
        name="both",
    )(ro, lo, own, other, *after)


def block_scales(values, first, held):
    lanes = lax.broadcasted_iota(jnp.int32, held.shape, 1)
    for p in range(values.shape[1] // 128):
        block = jnp.abs(values[:, p * 128 : (p + 1) * 128].astype(F32))
        largest = jnp.max(block, axis=1, keepdims=True) / 1.5
        held = jnp.where(lanes == first + p, largest, held)
    return held


OUTPUTS = [
    jax.ShapeDtypeStruct((3, 2, 64, WIDTH), BF16),
    jax.ShapeDtypeStruct((3, 2, BLOCKS, 64), F32),
]


def last_kernel(lo_ref, x_ref, *refs):
    o_ref, s_ref, turned, held = refs[-4:]
    step = pl.program_id(0)
    tile = o_ref.shape[3]
    stride = 136

    @pl.when(step == 0)
    def _():
        for k in range(64):
            for half in range(2):
                turned[pl.ds(half * 64 + k, BLOCKS, stride=stride), :] = x_ref[
                    2 * k + half
                ].astype(F32)

    first = step * (tile // 128)
    x = jnp.concatenate(
        [
            turned[pl.ds(pl.multiple_of((first + p) * stride, 8), 128), :].astype(BF16)
            for p in range(tile // 128)
        ],
        axis=1,
    )
    values = matmul(lo_ref[...], x).astype(BF16)
    o_ref[...] = values.reshape(1, 2, 64, tile)
    scales = block_scales(values, first, held[...])
    held[...] = scales
    flat = scales.T
    s_ref[0, 0] = flat[:BLOCKS, :64]
    s_ref[0, 1] = flat[:BLOCKS, 64:]


def last(x, lo, matrix, rotated, scales):
    tile = 1792
    return pl.pallas_call(
        last_kernel,
        grid=(WIDTH // tile,),
        in_specs=[
            pl.BlockSpec((128, 128), lambda i: (0, 0)),
            pl.BlockSpec((128, BLOCKS, 128), lambda i: (0, 0, 0)),
            ORDER,
            ORDER,
        ],
        out_specs=[
            pl.BlockSpec((1, 2, 64, tile), lambda i: (matrix, 0, 0, i)),
            pl.BlockSpec((1, 2, BLOCKS, 64), lambda i: (matrix, 0, 0, 0)),
        ],
        out_shape=OUTPUTS,
        scratch_shapes=[
            pltpu.VMEM((BLOCKS * 136, 128), F32),
            pltpu.VMEM((128, 128), F32),
        ],
        input_output_aliases={2: 0, 3: 1},
        compiler_params=pltpu.CompilerParams(vmem_limit_bytes=VMEM),
        cost_estimate=cost(2 * 128 * 128 * WIDTH, 2),
        name=f"last{matrix}",
    )(lo, x, rotated, scales)


def place_kernel(flip_ref, own_ref, other_ref, o_ref, s_ref, held):
    tile = o_ref.shape[3]
    lanes = pl.program_id(1) * (tile // 128)

    def put(ref):
        values = ref[...]
        o_ref[...] = values.reshape(1, 1, 64, tile)
        scales = block_scales(values, lanes, held[...])
        held[...] = scales
        s_ref[0, 0] = scales.T[:BLOCKS]

    pl.when(pl.program_id(0) == flip_ref[0])(lambda: put(own_ref))
    pl.when(pl.program_id(0) != flip_ref[0])(lambda: put(other_ref))


def place(own, other, flip):
    tile = 1792
    return pl.pallas_call(
        place_kernel,
        grid_spec=pltpu.PrefetchScalarGridSpec(
            num_scalar_prefetch=1,
            grid=(2, WIDTH // tile),
            in_specs=[pl.BlockSpec((64, tile), lambda h, i, flip: (0, i))] * 2,
            out_specs=[
                pl.BlockSpec((1, 1, 64, tile), lambda h, i, flip: (0, h, 0, i)),
                pl.BlockSpec((1, 1, BLOCKS, 64), lambda h, i, flip: (0, h, 0, 0)),
            ],
            scratch_shapes=[pltpu.VMEM((64, 128), F32)],
        ),
        out_shape=OUTPUTS,
        compiler_params=pltpu.CompilerParams(vmem_limit_bytes=VMEM),
        cost_estimate=cost(128 * WIDTH, 2),
        name="place",
    )(flip, own, other)


def gate(x, after):
    return pl.pallas_call(
        lambda *refs: None,
        in_specs=[ORDER] * (1 + len(after)),
        out_specs=ORDER,
        out_shape=jax.ShapeDtypeStruct(x.shape, x.dtype),
        input_output_aliases={0: 0},
        cost_estimate=pl.CostEstimate(flops=128, bytes_accessed=1024, transcendentals=0),
        name="gate",
    )(x, *after)


def swap(x, axis):
    return lax.ppermute(x, axis, [(0, 1), (1, 0)])


def exchange(x):
    return lax.all_to_all(x, (XH, Y, Z, XL), split_axis=0, concat_axis=0, tiled=True)


def local(weights, left_outer, left_inner, right_outer, right_inner):
    xl, core = lax.axis_index(XL), lax.axis_index(CORE)
    flip = jnp.full((1,), xl, jnp.int32)

    zero = jnp.zeros_like(left_outer)
    lo12 = jnp.concatenate(
        [
            jnp.concatenate([left_outer, zero], axis=1),
            jnp.concatenate([zero, left_outer], axis=1),
        ],
        axis=0,
    )

    ro = right_outer.reshape(2, 2, BLOCKS, 2, 2, BLOCKS)
    ro = jnp.where(core == 0, ro[:, 0], ro[:, 1, :, :, ::-1])
    ro = ro.transpose(0, 1, 3, 2, 4)
    ro0 = jnp.where(xl == 0, ro, ro[::-1]).reshape(2 * BLOCKS, 4 * BLOCKS)
    ro12 = jnp.where(xl == 0, ro, ro[:, :, :, ::-1]).reshape(2 * BLOCKS, 4 * BLOCKS)

    keep1, send1 = inner(weights, 1, flip, left_inner, right_inner, 2)
    (sent0,) = inner(weights, 0, flip, left_inner, right_inner, 1, [keep1])
    keep2, send2 = inner(weights, 2, flip, left_inner, right_inner, 2, [sent0])
    came0 = exchange(sent0)

    came1 = swap(send1, XL)
    keep1 = gate(keep1, [came1])
    sent1 = right([keep1, came1, swap(keep1, CORE), swap(came1, CORE)], ro12, [keep2])
    came2 = swap(send2, XL)
    keep2 = gate(keep2, [came2])

    came0 = gate(came0, [sent1, came2])
    own0, send0 = both(came0, swap(came0, CORE), ro0, left_outer)
    rotated, scales = place(own0, swap(send0, XL), flip)
    sent2 = right([keep2, came2, swap(keep2, CORE), swap(came2, CORE)], ro12, [scales])
    rotated, scales = last(exchange(sent1), lo12, 1, rotated, scales)
    rotated, scales = last(exchange(sent2), lo12, 2, rotated, scales)
    return rotated, scales.transpose(0, 1, 3, 2)


def solution(mesh):
    fine = Mesh(np.asarray(mesh.devices).reshape(SIZES), AXES)
    row, col = (XH, Y, Z), (XL, CORE)
    return jax.shard_map(
        local,
        mesh=fine,
        in_specs=(P(None, row, col), P(), P(), P(), P()),
        out_specs=(P(None, row, None, col), P(None, row, None, col)),
        check_vma=False,
    )
```

profile of v0, /device:TPU:1, one launch (start us, length us, event | category | flops | bytes accessed | tf_op | source)
XLA Modules:
  0.0 202.8 jit_solution(9938132911011481436)
XLA Ops:
  0.6 5.5 %inner1.1 = (bf16[64,56,128]{2,1,0:T(8,128)(2,1)}, bf16[64,56,128]{2,1,0:T(8,128)(2,1)}) custom-call(s32[1]{0:T(128)} %bitcast.3.xl_ref.flip_ref, bf16[3,128,7168]{2,1,0:T(8,128)(2,1)} %w_ref.5, bf16[128,128]{1,0:T(8,128)(2,1)} %li_ref.5, bf16[128,128]{1,0:T(8,128)(2,1)} %ri_ref.5), custom_call_target="tpu_custom_call" | custom-call | flops 469762048 | bytes 3670016 | tf_op jit(solution)/shard_map/inner1/pallas_call | solution.py:105
  6.1 2.1 %collective-permute-start.3 = (bf16[64,56,128]{2,1,0:T(8,128)(2,1)}, bf16[64,56,128]{2,1,0:T(8,128)(2,1)}, u32[]{:S(2)}, u32[]{:S(2)}) collective-permute-start(bf16[64,56,128]{2,1,0:T(8,128)(2,1)} %get-tuple-element.17), channel_id=1, source_target_pairs={{0,2},{2,0},{1,3},{3,1},{4,6},{6,4},{5,7},{7,5},{8,10},{10,8},{9,1... | collective-permute-start | bytes 2752520 | tf_op jit(solution)/shard_map/ppermute | solution.py:336
  8.2 5.4 %inner0.1.refs_0_ = bf16[128,56,128]{2,1,0:T(8,128)(2,1)} custom-call(s32[1]{0:T(128)} %bitcast.3.xl_ref.flip_ref, bf16[3,128,7168]{2,1,0:T(8,128)(2,1)} %w_ref.5, bf16[128,128]{1,0:T(8,128)(2,1)} %li_ref.5, bf16[128,128]{1,0:T(8,128)(2,1)} %ri_ref.5, bf16[64,56,128]{2,1,0:T(8,128)(2,1)} %get-tuple-element.14.refs_0_), custom_call_target="tpu_custom_call" | custom-call | flops 469762048 | bytes 3670016 | tf_op jit(solution)/shard_map/inner0/pallas_call | solution.py:105
  13.7 15.2 %all-to-all-start = ((bf16[128,56,128]{2,1,0:T(8,128)(2,1)}), bf16[128,56,128]{2,1,0:T(8,128)(2,1)S(1)}, u32[]{:S(2)}, u32[]{:S(2)}) async-start(bf16[128,56,128]{2,1,0:T(8,128)(2,1)} %inner0.1.refs_0_), calls=%async_computation | async-start | bytes 3670016 | tf_op jit(solution)/shard_map/all_to_all | solution.py:340
  28.9 1.3 collective-permute-start.5
  30.4 5.4 %inner2.1 = (bf16[64,56,128]{2,1,0:T(8,128)(2,1)}, bf16[64,56,128]{2,1,0:T(8,128)(2,1)}) custom-call(s32[1]{0:T(128)} %bitcast.3.xl_ref.flip_ref, bf16[3,128,7168]{2,1,0:T(8,128)(2,1)} %w_ref.5, bf16[128,128]{1,0:T(8,128)(2,1)} %li_ref.5, bf16[128,128]{1,0:T(8,128)(2,1)} %ri_ref.5, bf16[128,56,128]{2,1,0:T(8,128)(2,1)} %inner0.1.refs_0_), custom_call_target="tpu_custom_call" | custom-call | flops 469762048 | bytes 3670016 | tf_op jit(solution)/shard_map/inner2/pallas_call | solution.py:105
  35.8 1.3 collective-permute-start
  37.1 0.2 reshape.15
  37.2 0.2 fusion.4
  37.5 0.1 fusion
  37.6 0.6 rev.10
  38.2 0.2 broadcast_select_fusion.1
  38.6 1.2 copy-done.5
  39.8 4.0 %right.2.refs_1_ = bf16[128,56,128]{2,1,0:T(8,128)(2,1)S(1)} custom-call(bf16[112,224]{1,0:T(8,128)(2,1)S(1)} %reshape.16.ro_ref, bf16[64,56,128]{2,1,0:T(8,128)(2,1)S(1)} %copy-done.3, bf16[64,56,128]{2,1,0:T(8,128)(2,1)} %collective-permute-done.3.refs_1_, bf16[64,56,128]{2,1,0:T(8,128)(2,1)} %collective-permute-done.4.refs_2_, ...), custom_call_target="tpu_custom_call" | custom-call | flops 23060000768 | bytes 5505024 | tf_op jit(solution)/shard_map/right/pallas_call | solution.py:159
  43.8 1.2 copy-done.2
  45.0 26.8 %collective-permute-done.refs_1_.refs_2_ = bf16[64,56,128]{2,1,0:T(8,128)(2,1)} collective-permute-done((bf16[64,56,128]{2,1,0:T(8,128)(2,1)}, bf16[64,56,128]{2,1,0:T(8,128)(2,1)}, u32[]{:S(2)}, u32[]{:S(2)}) %collective-permute-start) | collective-permute-done | bytes 917536 | tf_op jit(solution)/shard_map/ppermute | solution.py:336
  71.9 1.9 all-to-all-done.refs_0_
  73.8 1.2 copy-done
  75.0 2.7 %collective-permute-start.6 = (bf16[128,56,128]{2,1,0:T(8,128)(2,1)}, bf16[128,56,128]{2,1,0:T(8,128)(2,1)}, u32[]{:S(2)}, u32[]{:S(2)}) collective-permute-start(bf16[128,56,128]{2,1,0:T(8,128)(2,1)} %gate.5.own_ref), channel_id=1, source_target_pairs={{0,1},{1,0},{2,3},{3,2},{4,5},{5,4},{6,7},{7,6},{8,9},{9,8},{10,11... | collective-permute-start | bytes 5505032 | tf_op jit(solution)/shard_map/ppermute | solution.py:336
  77.6 13.0 %all-to-all-start.2 = ((bf16[128,56,128]{2,1,0:T(8,128)(2,1)}), bf16[128,56,128]{2,1,0:T(8,128)(2,1)}, u32[]{:S(2)}, u32[]{:S(2)}) async-start(bf16[128,56,128]{2,1,0:T(8,128)(2,1)} %copy-done.2), calls=%async_computation.2 | async-start | bytes 3670016 | tf_op jit(solution)/shard_map/all_to_all | solution.py:340
  90.8 3.8 %both.1 = (bf16[64,7168]{1,0:T(8,128)(2,1)S(1)}, bf16[64,7168]{1,0:T(8,128)(2,1)}) custom-call(bf16[112,224]{1,0:T(8,128)(2,1)S(1)} %reshape.17.ro_ref, bf16[64,64]{1,0:T(8,128)(2,1)S(1)} %copy-done.8, bf16[128,56,128]{2,1,0:T(8,128)(2,1)S(1)} %copy-done.1, bf16[128,56,128]{2,1,0:T(8,128)(2,1)} %collective-permute-done.6.other_ref), custom_call_target="tpu_custom_call" | custom-call | flops 256901120 | bytes 5505024 | tf_op jit(solution)/shard_map/both/pallas_call | solution.py:202
  94.6 0.5 collective-permute-start.7
  95.1 1.0 collective-permute-start.2
  96.1 35.9 %collective-permute-done.7.other_ref = bf16[64,7168]{1,0:T(8,128)(2,1)S(1)} collective-permute-done((bf16[64,7168]{1,0:T(8,128)(2,1)}, bf16[64,7168]{1,0:T(8,128)(2,1)S(1)}, u32[]{:S(2)}, u32[]{:S(2)}) %collective-permute-start.7) | collective-permute-done | bytes 917536 | tf_op jit(solution)/shard_map/ppermute | solution.py:336
  132.0 4.3 %place.1 = (bf16[3,2,64,7168]{3,2,1,0:T(8,128)(2,1)}, f32[3,2,56,64]{3,2,1,0:T(8,128)}) custom-call(s32[1]{0:T(128)} %bitcast.3.xl_ref.flip_ref, bf16[64,7168]{1,0:T(8,128)(2,1)S(1)} %get-tuple-element.18.own_ref, bf16[64,7168]{1,0:T(8,128)(2,1)S(1)} %collective-permute-done.7.other_ref), custom_call_target="tpu_custom_call" | custom-call | flops 917504 | bytes 3670016 | tf_op jit(solution)/shard_map/place/pallas_call | solution.py:304
  136.4 0.9 copy-done.7
  137.3 3.7 %right.3 = bf16[128,56,128]{2,1,0:T(8,128)(2,1)S(1)} custom-call(bf16[112,224]{1,0:T(8,128)(2,1)S(1)} %reshape.16.ro_ref, bf16[64,56,128]{2,1,0:T(8,128)(2,1)S(1)} %copy-done.6, bf16[64,56,128]{2,1,0:T(8,128)(2,1)} %collective-permute-done.refs_1_.refs_2_, bf16[64,56,128]{2,1,0:T(8,128)(2,1)S(1)} %collective-permute-done.1.refs_2_, ...), custom_call_target="tpu_custom_call" | custom-call | flops 23060000768 | bytes 5505024 | tf_op jit(solution)/shard_map/right/pallas_call | solution.py:159
  141.0 1.3 copy-done.4
  142.3 11.9 %all-to-all-start.1 = ((bf16[128,56,128]{2,1,0:T(8,128)(2,1)}), bf16[128,56,128]{2,1,0:T(8,128)(2,1)S(1)}, u32[]{:S(2)}, u32[]{:S(2)}) async-start(bf16[128,56,128]{2,1,0:T(8,128)(2,1)} %copy-done.4), calls=%async_computation.1 | async-start | bytes 3670016 | tf_op jit(solution)/shard_map/all_to_all | solution.py:340
  154.3 5.4 %last1.1 = (bf16[3,2,64,7168]{3,2,1,0:T(8,128)(2,1)}, f32[3,2,56,64]{3,2,1,0:T(8,128)}) custom-call(bf16[128,128]{1,0:T(8,128)(2,1)S(1)} %fusion.3.lo_ref, bf16[128,56,128]{2,1,0:T(8,128)(2,1)} %all-to-all-done.2.x_ref, bf16[3,2,64,7168]{3,2,1,0:T(8,128)(2,1)} %get-tuple-element.21.refs_0_, ...), custom_call_target="tpu_custom_call", output_to_operand_aliasing={{0}: (2, {}), {1}: (3, {})} | custom-call | flops 234881024 | bytes 3670016 | tf_op jit(solution)/shard_map/last1/pallas_call | solution.py:262
  159.7 39.2 %all-to-all-done.1.x_ref = bf16[128,56,128]{2,1,0:T(8,128)(2,1)S(1)} async-done(((bf16[128,56,128]{2,1,0:T(8,128)(2,1)}), bf16[128,56,128]{2,1,0:T(8,128)(2,1)S(1)}, u32[]{:S(2)}, u32[]{:S(2)}) %all-to-all-start.1) | async-done | bytes 1835040 | tf_op jit(solution)/shard_map/all_to_all | solution.py:340
  198.9 3.9 %last2.1 = (bf16[3,2,64,7168]{3,2,1,0:T(8,128)(2,1)}, f32[3,2,56,64]{3,2,1,0:T(8,128)}) custom-call(bf16[128,128]{1,0:T(8,128)(2,1)S(1)} %fusion.3.lo_ref, bf16[128,56,128]{2,1,0:T(8,128)(2,1)S(1)} %all-to-all-done.1.x_ref, bf16[3,2,64,7168]{3,2,1,0:T(8,128)(2,1)} %get-tuple-element.22.refs_0_, ...), custom_call_target="tpu_custom_call", output_to_operand_aliasing={{0}: (2, {}), {1}: (3, {})} | custom-call | flops 234881024 | bytes 3670016 | tf_op jit(solution)/shard_map/last2/pallas_call | solution.py:262
  (31 shorter events, 0.6 us)
Async XLA Ops:
  6.1 22.8 %collective-permute-start.3 = (bf16[64,56,128]{2,1,0:T(8,128)(2,1)}, bf16[64,56,128]{2,1,0:T(8,128)(2,1)}, u32[]{:S(2)}, u32[]{:S(2)}) collective-permute-start(bf16[64,56,128]{2,1,0:T(8,128)(2,1)} %get-tuple-element.17), channel_id=1, source_target_pairs={{0,2},{2,0},{1,3},{3,1},{4,6},{6,4},{5,7},{7,5},{8,10},{10,8},{9,1... | collective-permute-start | bytes 2752520 | tf_op jit(solution)/shard_map/ppermute | solution.py:336
  13.7 60.1 %all-to-all-start = ((bf16[128,56,128]{2,1,0:T(8,128)(2,1)}), bf16[128,56,128]{2,1,0:T(8,128)(2,1)S(1)}, u32[]{:S(2)}, u32[]{:S(2)}) async-start(bf16[128,56,128]{2,1,0:T(8,128)(2,1)} %inner0.1.refs_0_), calls=%async_computation | async-start | bytes 3670016 | tf_op jit(solution)/shard_map/all_to_all | solution.py:340
  28.9 9.7 %collective-permute-start.5 = (bf16[64,56,128]{2,1,0:T(8,128)(2,1)}, bf16[64,56,128]{2,1,0:T(8,128)(2,1)}, u32[]{:S(2)}, u32[]{:S(2)}) collective-permute-start(bf16[64,56,128]{2,1,0:T(8,128)(2,1)} %collective-permute-done.3.refs_1_), channel_id=1, source_target_pairs={{0,1},{1,0},{2,3},{3,2},{4,5},{5,4},{6,7},{7,6},{8,9},{9,8},{10,11... | collective-permute-start | bytes 2752520 | tf_op jit(solution)/shard_map/ppermute | solution.py:336
  30.2 6.8 %copy-start.9 = (bf16[224,224]{1,0:T(8,128)(2,1)S(1)}, bf16[224,224]{1,0:T(8,128)(2,1)}, u32[]{:S(2)}) copy-start(bf16[224,224]{1,0:T(8,128)(2,1)} %param.8) | copy-start | bytes 301060
  30.2 8.3 %collective-permute-start.4 = (bf16[64,56,128]{2,1,0:T(8,128)(2,1)}, bf16[64,56,128]{2,1,0:T(8,128)(2,1)}, u32[]{:S(2)}, u32[]{:S(2)}) collective-permute-start(bf16[64,56,128]{2,1,0:T(8,128)(2,1)} %gate.4.refs_0_), channel_id=1, source_target_pairs={{0,1},{1,0},{2,3},{3,2},{4,5},{5,4},{6,7},{7,6},{8,9},{9,8},{10,11... | collective-permute-start | bytes 2752520 | tf_op jit(solution)/shard_map/ppermute | solution.py:336
  35.8 2.8 %copy-start.3 = (bf16[64,56,128]{2,1,0:T(8,128)(2,1)S(1)}, bf16[64,56,128]{2,1,0:T(8,128)(2,1)}, u32[]{:S(2)}) copy-start(bf16[64,56,128]{2,1,0:T(8,128)(2,1)} %gate.4.refs_0_) | copy-start | bytes 2752516
  35.8 36.1 %collective-permute-start = (bf16[64,56,128]{2,1,0:T(8,128)(2,1)}, bf16[64,56,128]{2,1,0:T(8,128)(2,1)}, u32[]{:S(2)}, u32[]{:S(2)}) collective-permute-start(bf16[64,56,128]{2,1,0:T(8,128)(2,1)} %get-tuple-element.16), channel_id=1, source_target_pairs={{0,2},{2,0},{1,3},{3,1},{4,6},{6,4},{5,7},{7,5},{8,10},{10,8},{9,1... | collective-permute-start | bytes 2752520 | tf_op jit(solution)/shard_map/ppermute | solution.py:336
  38.6 1.2 copy-start.5
  43.8 1.3 copy-start.2
  73.8 1.2 copy-start
  75.0 15.8 %copy-start.1 = (bf16[128,56,128]{2,1,0:T(8,128)(2,1)S(1)}, bf16[128,56,128]{2,1,0:T(8,128)(2,1)}, u32[]{:S(2)}) copy-start(bf16[128,56,128]{2,1,0:T(8,128)(2,1)} %gate.5.own_ref) | copy-start | bytes 5505028
  75.0 15.8 %copy-start.8 = (bf16[64,64]{1,0:T(8,128)(2,1)S(1)}, bf16[64,64]{1,0:T(8,128)(2,1)}, u32[]{:S(2)}) copy-start(bf16[64,64]{1,0:T(8,128)(2,1)} %lo_ref.1) | copy-start | bytes 24580
  75.0 15.8 %collective-permute-start.6 = (bf16[128,56,128]{2,1,0:T(8,128)(2,1)}, bf16[128,56,128]{2,1,0:T(8,128)(2,1)}, u32[]{:S(2)}, u32[]{:S(2)}) collective-permute-start(bf16[128,56,128]{2,1,0:T(8,128)(2,1)} %gate.5.own_ref), channel_id=1, source_target_pairs={{0,1},{1,0},{2,3},{3,2},{4,5},{5,4},{6,7},{7,6},{8,9},{9,8},{10,11... | collective-permute-start | bytes 5505032 | tf_op jit(solution)/shard_map/ppermute | solution.py:336
  77.6 64.6 %all-to-all-start.2 = ((bf16[128,56,128]{2,1,0:T(8,128)(2,1)}), bf16[128,56,128]{2,1,0:T(8,128)(2,1)}, u32[]{:S(2)}, u32[]{:S(2)}) async-start(bf16[128,56,128]{2,1,0:T(8,128)(2,1)} %copy-done.2), calls=%async_computation.2 | async-start | bytes 3670016 | tf_op jit(solution)/shard_map/all_to_all | solution.py:340
  94.6 37.4 %collective-permute-start.7 = (bf16[64,7168]{1,0:T(8,128)(2,1)}, bf16[64,7168]{1,0:T(8,128)(2,1)S(1)}, u32[]{:S(2)}, u32[]{:S(2)}) collective-permute-start(bf16[64,7168]{1,0:T(8,128)(2,1)} %get-tuple-element.19), channel_id=1, source_target_pairs={{0,2},{2,0},{1,3},{3,1},{4,6},{6,4},{5,7},{7,5},{8,10},{10,8},{9,1... | collective-permute-start | bytes 2752520 | tf_op jit(solution)/shard_map/ppermute | solution.py:336
  95.1 41.2 %collective-permute-start.2 = (bf16[64,56,128]{2,1,0:T(8,128)(2,1)}, bf16[64,56,128]{2,1,0:T(8,128)(2,1)}, u32[]{:S(2)}, u32[]{:S(2)}) collective-permute-start(bf16[64,56,128]{2,1,0:T(8,128)(2,1)} %collective-permute-done.refs_1_.refs_2_), channel_id=1, source_target_pairs={{0,1},{1,0},{2,3},{3,2},{4,5},{5,4},{6,7},{7,6},{8,9},{9,8},{10,11... | collective-permute-start | bytes 2752520 | tf_op jit(solution)/shard_map/ppermute | solution.py:336
  96.1 40.2 %copy-start.6 = (bf16[64,56,128]{2,1,0:T(8,128)(2,1)S(1)}, bf16[64,56,128]{2,1,0:T(8,128)(2,1)}, u32[]{:S(2)}) copy-start(bf16[64,56,128]{2,1,0:T(8,128)(2,1)} %gate.3.refs_0_) | copy-start | bytes 2752516
  96.1 40.2 %collective-permute-start.1 = (bf16[64,56,128]{2,1,0:T(8,128)(2,1)}, bf16[64,56,128]{2,1,0:T(8,128)(2,1)S(1)}, u32[]{:S(2)}, u32[]{:S(2)}) collective-permute-start(bf16[64,56,128]{2,1,0:T(8,128)(2,1)} %gate.3.refs_0_), channel_id=1, source_target_pairs={{0,1},{1,0},{2,3},{3,2},{4,5},{5,4},{6,7},{7,6},{8,9},{9,8},{10,11... | collective-permute-start | bytes 2752520 | tf_op jit(solution)/shard_map/ppermute | solution.py:336
  136.3 0.9 copy-start.7
  141.0 1.3 copy-start.4
  142.3 56.6 %all-to-all-start.1 = ((bf16[128,56,128]{2,1,0:T(8,128)(2,1)}), bf16[128,56,128]{2,1,0:T(8,128)(2,1)S(1)}, u32[]{:S(2)}, u32[]{:S(2)}) async-start(bf16[128,56,128]{2,1,0:T(8,128)(2,1)} %copy-done.4), calls=%async_computation.1 | async-start | bytes 3670016 | tf_op jit(solution)/shard_map/all_to_all | solution.py:340
where the time goes:
time: 204 us; the launch traced here: 203 us
  waiting for transfers between devices  104 us (51%)
  starting transfers between devices  49.1 us (24%)
  Pallas kernels  41.4 us (20%)
  local copies, waits for them, and re-layouts  7.08 us (3%)
    ppermute x8, waiting for transfers between devices, swap(): return lax.ppermute(x, axis, [(0, 1), (1, 0)])  62.7 us
    all_to_all x3, waiting for transfers between devices, exchange(): lax.all_to_all(x, (XH, Y, Z, XL), split_axis=0, concat_axis=0, tiled=True)  41.1 us
    all_to_all x3, starting transfers between devices, exchange(): lax.all_to_all(x, (XH, Y, Z, XL), split_axis=0, concat_axis=0, tiled=True)  40.1 us
    pallas_call x3, Pallas kernels, inner(): pl.pallas_call(functools.partial(inner_kernel, matrix, cuts), in_specs=[p...  16.3 us
    pallas_call x2, Pallas kernels, last(): pl.pallas_call(last_kernel, grid=(WIDTH // tile,), in_specs=[pl.BlockSpec...  9.28 us
    ppermute x8, starting transfers between devices, swap(): return lax.ppermute(x, axis, [(0, 1), (1, 0)])  9.02 us
    pallas_call x2, Pallas kernels, right(): pl.pallas_call(right_kernel, in_specs=[WHOLE] * 5 + [ORDER] * len(after),...  7.75 us
    unnamed x21, local copies, waits for them, and re-layouts  5.92 us
  transfers between devices with their start and end apart: 11, of which 4 were waited for; matrix products, arithmetic and copies ran while one was open for 1% of the time, Pallas kernels for 16%

commit v1 on v0

v1 whole, which is shorter than its diff:
```python
import functools

import jax
import jax.numpy as jnp
import numpy as np
from jax import lax
from jax.experimental import pallas as pl
from jax.experimental.pallas import tpu as pltpu
from jax.sharding import Mesh
from jax.sharding import PartitionSpec as P

BF16 = jnp.bfloat16
F32 = jnp.float32
XH, Y, Z, XL, CORE = "xh", "y", "z", "xl", "core"
AXES = (XH, Y, Z, XL, CORE)
SIZES = (2, 4, 8, 2, 2)
WIDTH = 7168
BLOCKS = 56
VMEM = 24 * 1024 * 1024
INNER_VMEM = 60 * 1024 * 1024
MICROS = 20
WHOLE = pl.BlockSpec(memory_space=pltpu.VMEM)
ORDER = pl.BlockSpec(memory_space=pl.ANY)


def matmul(left, right):
    return jnp.dot(left, right, preferred_element_type=F32)


def blocks_of(count):
    return jax.ShapeDtypeStruct((count, BLOCKS, 128), BF16)


def cost(flops, passes):
    return pl.CostEstimate(
        flops=flops, bytes_accessed=passes * 128 * WIDTH * 2, transcendentals=0
    )


def inner_kernel(matrices, outs, place_ref, w_ref, li_ref, ri_ref, *refs):
    o_refs, (held, turned, packed, sems, out_sems) = refs[-5 - outs : -5], refs[-5:]
    tiles = 4
    tile = WIDTH // tiles
    copies = [
        pltpu.make_async_copy(
            w_ref.at[matrix, :, pl.ds(t * tile, tile)],
            held.at[at * tiles + t],
            sems.at[at * tiles + t],
        )
        for at, matrix in enumerate(matrices)
        for t in range(tiles)
    ]
    for copy in copies:
        copy.start()
    ri = ri_ref[...]
    zero = jnp.zeros_like(ri)
    pair = jnp.concatenate(
        [
            jnp.concatenate([ri, zero], axis=1),
            jnp.concatenate([zero, ri], axis=1),
        ],
        axis=0,
    )
    li = li_ref[...]
    parts = []
    for place in range(len(matrices)):
        for t in range(tiles):
            which = place * tiles + t
            copies[which].wait()
            pairs = tile // 256
            stacked = jnp.concatenate(
                [held[which, :, c * 256 : (c + 1) * 256] for c in range(pairs)], axis=0
            )
            first = lax.dot_general(
                stacked, pair, (((1,), (1,)), ((), ())), preferred_element_type=F32
            ).astype(BF16)
            first = jnp.concatenate(
                [first[c * 128 : (c + 1) * 128] for c in range(pairs)], axis=1
            )
            second = matmul(li, first)
            for p in range(tile // 128):
                turned[pl.ds(t * (tile // 128) + p, 128, stride=BLOCKS), :] = second[
                    :, p * 128 : (p + 1) * 128
                ]
        for part in range(4):
            half = 1 - part // 2
            for r in range(32):
                if outs == 1:
                    to = part * 32 + r
                    row = to * BLOCKS
                else:
                    to = half * 64 + part % 2 * 32 + r
                    at = (place_ref[0] ^ (part % 2)) * 32 + r
                    row = pl.multiple_of((2 * at + (place_ref[1] ^ half)) * BLOCKS, 8)
                packed[place, to] = turned[pl.ds(row, BLOCKS), :].astype(BF16)
            if outs == 1:
                here, there = part * 32, o_refs[0].at[pl.ds(part * 32, 32), place]
            else:
                at = part % 2 * 32
                here, there = half * 64 + at, o_refs[half].at[pl.ds(at, 32)]
            parts.append(
                pltpu.make_async_copy(
                    packed.at[place, pl.ds(here, 32)], there, out_sems.at[len(parts)]
                )
            )
            parts[-1].start()
    for copy in parts:
        copy.wait()


def inner(weights, matrices, where, li, ri, shapes, after=()):
    hbm = pl.BlockSpec(memory_space=pltpu.HBM)
    count = len(matrices)
    return pl.pallas_call(
        functools.partial(inner_kernel, matrices, len(shapes)),
        in_specs=[pl.BlockSpec(memory_space=pltpu.SMEM), hbm, WHOLE, WHOLE]
        + [ORDER] * len(after),
        out_specs=[hbm] * len(shapes),
        out_shape=shapes,
        scratch_shapes=[
            pltpu.VMEM((4 * count, 128, WIDTH // 4), BF16),
            pltpu.VMEM((128 * BLOCKS, 128), F32),
            pltpu.VMEM((count, 128, BLOCKS, 128), BF16),
            pltpu.SemaphoreType.DMA((4 * count,)),
            pltpu.SemaphoreType.DMA((4 * count,)),
        ],
        compiler_params=pltpu.CompilerParams(vmem_limit_bytes=INNER_VMEM),
        cost_estimate=cost(4 * 128 * 128 * WIDTH, 2),
        name=f"inner{matrices[0]}",
    )(where, weights, li, ri, *after)


def mix_blocks(refs, rows, ro):
    columns = jnp.concatenate(
        [
            jnp.concatenate([ref[at].astype(F32) for ref, at in zip(refs, where)], axis=0)
            for where in rows
        ],
        axis=1,
    )
    return matmul(ro, columns.astype(BF16))


def right_kernel(ro_ref, *refs):
    sources, (packed, sems) = refs[:4], refs[-2:]
    o_refs = refs[-6:-2]
    ro = ro_ref[...]
    copies = []
    for first in range(0, 64, 4):
        rows = range(first, first + 4)
        mixed = mix_blocks(sources, [(r,) * 4 for r in rows], ro)
        for at, r in enumerate(rows):
            lanes = slice(at * 128, at * 128 + 128)
            for half in range(2):
                block = mixed[half * BLOCKS : (half + 1) * BLOCKS, lanes]
                packed[r // 32 * 2 + half, r % 32] = block.astype(BF16)
        if first % 32 == 28:
            for to in (first // 32 * 2, first // 32 * 2 + 1):
                copies.append(pltpu.make_async_copy(packed.at[to], o_refs[to], sems.at[to]))
                copies[-1].start()
    for copy in copies:
        copy.wait()


def right(sources, ro, after=()):
    return pl.pallas_call(
        right_kernel,
        in_specs=[WHOLE] * 5 + [ORDER] * len(after),
        out_specs=[pl.BlockSpec(memory_space=pltpu.HBM)] * 4,
        out_shape=[blocks_of(32)] * 4,
        scratch_shapes=[
            pltpu.VMEM((4, 32, BLOCKS, 128), BF16),
            pltpu.SemaphoreType.DMA((4,)),
        ],
        compiler_params=pltpu.CompilerParams(vmem_limit_bytes=VMEM),
        cost_estimate=cost(1153 * 10**6 * MICROS, 3),
        name="right",
    )(ro, *sources, *after)


def join_kernel(*refs):
    o_ref, packed, sems = refs[-3:]
    copies = []
    for part in range(4):
        rows = pl.ds(part * 8, 8)
        for row in range(part * 8, part * 8 + 8):
            for at, ref in enumerate(refs[:4]):
                packed[row, at] = ref[row]
        copies.append(
            pltpu.make_async_copy(packed.at[rows], o_ref.at[rows], sems.at[part])
        )
        copies[-1].start()
    for copy in copies:
        copy.wait()


def join(pieces):
    return pl.pallas_call(
        join_kernel,
        in_specs=[WHOLE] * 4,
        out_specs=pl.BlockSpec(memory_space=pltpu.HBM),
        out_shape=jax.ShapeDtypeStruct((32, 4, BLOCKS, 128), BF16),
        scratch_shapes=[
            pltpu.VMEM((32, 4, BLOCKS, 128), BF16),
            pltpu.SemaphoreType.DMA((4,)),
        ],
        compiler_params=pltpu.CompilerParams(vmem_limit_bytes=VMEM),
        cost_estimate=cost(0, 2),
        name="join",
    )(*pieces)


def both_kernel(matrix, ro_ref, lo_ref, own_ref, other_ref, *refs):
    o_refs, turned = refs[-3:-1], refs[-1]
    ro = ro_ref[...]
    sources = (own_ref, own_ref, other_ref, other_ref)
    stride = 72
    for first in range(0, 64, 4):
        rows = range(first, first + 4)
        where = [((2 * r, 0), (2 * r + 1, 0)) * 2 for r in rows]
        mixed = mix_blocks(sources, where, ro)
        for at, r in enumerate(rows):
            turned[pl.ds(r, 2 * BLOCKS, stride=stride), :] = mixed[
                :, at * 128 : at * 128 + 128
            ]
    lo = lo_ref[...]
    for half, ref in enumerate(o_refs):
        for first in range(0, BLOCKS, 14):
            x = jnp.concatenate(
                [
                    turned[
                        (half * BLOCKS + p) * stride : (half * BLOCKS + p) * stride + 64, :
                    ].astype(BF16)
                    for p in range(first, first + 14)
                ],
                axis=1,
            )
            ref[:, first * 128 : (first + 14) * 128] = matmul(lo, x).astype(BF16)


def both(own, other, matrix, ro, lo):
    fixed = lambda shape: pl.BlockSpec(shape, lambda i: (0,) * len(shape))
    blocks = pl.BlockSpec((128, 1, BLOCKS, 128), lambda i: (0, matrix, 0, 0))
    return pl.pallas_call(
        functools.partial(both_kernel, matrix),
        grid=(1,),
        in_specs=[fixed(ro.shape), fixed(lo.shape), blocks, blocks],
        out_specs=[fixed((64, WIDTH))] * 2,
        out_shape=[jax.ShapeDtypeStruct((64, WIDTH), BF16)] * 2,
        scratch_shapes=[pltpu.VMEM((2 * BLOCKS * 72, 128), F32)],
        compiler_params=pltpu.CompilerParams(vmem_limit_bytes=VMEM),
        cost_estimate=cost(10 * 64 * BLOCKS * WIDTH, 3),
        name=f"both{matrix}",
    )(ro, lo, own, other)


def block_scales(values, first, held):
    lanes = lax.broadcasted_iota(jnp.int32, held.shape, 1)
    for p in range(values.shape[1] // 128):
        block = jnp.abs(values[:, p * 128 : (p + 1) * 128].astype(F32))
        largest = jnp.max(block, axis=1, keepdims=True) / 1.5
        held = jnp.where(lanes == first + p, largest, held)
    return held


OUTPUTS = [
    jax.ShapeDtypeStruct((3, 2, 64, WIDTH), BF16),
    jax.ShapeDtypeStruct((3, 2, BLOCKS, 64), F32),
]


def last_kernel(lo_ref, x_ref, *refs):
    o_ref, s_ref, turned, held = refs[-4:]
    step = pl.program_id(0)
    tile = o_ref.shape[3]
    stride = 136

    @pl.when(step == 0)
    def _():
        for row in range(128):
            turned[pl.ds(row, BLOCKS, stride=stride), :] = x_ref[row].astype(F32)

    first = step * (tile // 128)
    x = jnp.concatenate(
        [
            turned[pl.ds(pl.multiple_of((first + p) * stride, 8), 128), :].astype(BF16)
            for p in range(tile // 128)
        ],
        axis=1,
    )
    values = matmul(lo_ref[...], x).astype(BF16)
    o_ref[...] = values.reshape(1, 2, 64, tile)
    scales = block_scales(values, first, held[...])
    held[...] = scales
    flat = scales.T
    s_ref[0, 0] = flat[:BLOCKS, :64]
    s_ref[0, 1] = flat[:BLOCKS, 64:]


def last(x, lo, matrix, rotated, scales):
    tile = 1792
    return pl.pallas_call(
        last_kernel,
        grid=(WIDTH // tile,),
        in_specs=[
            pl.BlockSpec((128, 128), lambda i: (0, 0)),
            pl.BlockSpec((128, BLOCKS, 128), lambda i: (0, 0, 0)),
            ORDER,
            ORDER,
        ],
        out_specs=[
            pl.BlockSpec((1, 2, 64, tile), lambda i: (matrix, 0, 0, i)),
            pl.BlockSpec((1, 2, BLOCKS, 64), lambda i: (matrix, 0, 0, 0)),
        ],
        out_shape=OUTPUTS,
        scratch_shapes=[
            pltpu.VMEM((BLOCKS * 136, 128), F32),
            pltpu.VMEM((128, 128), F32),
        ],
        input_output_aliases={2: 0, 3: 1},
        compiler_params=pltpu.CompilerParams(vmem_limit_bytes=VMEM),
        cost_estimate=cost(2 * 128 * 128 * WIDTH, 2),
        name=f"last{matrix}",
    )(lo, x, rotated, scales)


def place_kernel(half_ref, x_ref, *refs):
    o_ref, s_ref, held = refs[-3:]
    tile = o_ref.shape[3]
    values = x_ref[...]
    o_ref[...] = values.reshape(1, 1, 64, tile)
    scales = block_scales(values, pl.program_id(0) * (tile // 128), held[...])
    held[...] = scales
    s_ref[0, 0] = scales.T[:BLOCKS]


def place(x, half, matrix, into=()):
    tile = 1792
    return pl.pallas_call(
        place_kernel,
        grid_spec=pltpu.PrefetchScalarGridSpec(
            num_scalar_prefetch=1,
            grid=(WIDTH // tile,),
            in_specs=[pl.BlockSpec((64, tile), lambda i, half: (0, i))]
            + [ORDER] * len(into),
            out_specs=[
                pl.BlockSpec((1, 1, 64, tile), lambda i, half: (matrix, half[0], 0, i)),
                pl.BlockSpec((1, 1, BLOCKS, 64), lambda i, half: (matrix, half[0], 0, 0)),
            ],
            scratch_shapes=[pltpu.VMEM((64, 128), F32)],
        ),
        out_shape=OUTPUTS,
        input_output_aliases={2: 0, 3: 1} if into else {},
        compiler_params=pltpu.CompilerParams(vmem_limit_bytes=VMEM),
        cost_estimate=cost(64 * WIDTH, 1),
        name=f"place{matrix}",
    )(half, x, *into)


def gate(x, after):
    return pl.pallas_call(
        lambda *refs: None,
        in_specs=[ORDER] * (1 + len(after)),
        out_specs=ORDER,
        out_shape=jax.ShapeDtypeStruct(x.shape, x.dtype),
        input_output_aliases={0: 0},
        cost_estimate=pl.CostEstimate(flops=128, bytes_accessed=1024, transcendentals=0),
        name="gate",
    )(x, *after)


def swap(x, axis):
    return lax.ppermute(x, axis, [(0, 1), (1, 0)])


def local(weights, left_outer, left_inner, right_outer, right_inner):
    xh, xl, core = lax.axis_index(XH), lax.axis_index(XL), lax.axis_index(CORE)
    where = jnp.stack([xh, xl]).astype(jnp.int32)
    own_half = where[1:]

    lo = left_outer.reshape(64, 2, 32)
    lo = jnp.where(xh == 0, lo, lo[:, ::-1]).transpose(0, 2, 1)
    same = jnp.eye(2, dtype=BF16)
    same = jnp.where(xl == 0, same, same[::-1])
    lo2 = lo.reshape(1, 64, 32, 2, 1) * same.reshape(2, 1, 1, 1, 2)
    lo2 = lo2.reshape(128, 128)

    ro = right_outer.reshape(2, 2, BLOCKS, 2, 2, BLOCKS)
    ro = jnp.where(core == 0, ro[:, 0], ro[:, 1, :, :, ::-1])
    ro = ro.transpose(0, 1, 3, 2, 4)
    ro01 = jnp.where(xl == 0, ro, ro[::-1]).reshape(2 * BLOCKS, 4 * BLOCKS)
    ro2 = jnp.where(xl == 0, ro, ro[::-1, :, :, ::-1]).reshape(2 * BLOCKS, 4 * BLOCKS)

    sent01_shape = jax.ShapeDtypeStruct((128, 2, BLOCKS, 128), BF16)
    (sent01,) = inner(weights, (0, 1), where, left_inner, right_inner, [sent01_shape])
    came01 = lax.all_to_all(sent01, (XH, Y, Z, XL), 0, 0, tiled=True)

    keep2, send2 = inner(
        weights, (2,), where, left_inner, right_inner, [blocks_of(64)] * 2, [sent01]
    )
    came2 = swap(send2, XL)
    keep2 = gate(keep2, [came2])
    planes = right([keep2, came2, swap(keep2, CORE), swap(came2, CORE)], ro2)
    planes = [planes[0]] + [
        lax.ppermute(planes[d], (XH, XL), [(i, i ^ d) for i in range(4)])
        for d in range(1, 4)
    ]
    sent2 = join(planes)
    came01 = gate(came01, [sent2])
    came2 = lax.all_to_all(sent2, (Y, Z), 0, 0, tiled=True)

    other01 = swap(came01, CORE)
    own0, send0 = both(came01, other01, 0, ro01, left_outer)
    own1, send1 = both(came01, other01, 1, ro01, left_outer)
    outputs = place(own0, own_half, 0)
    outputs = place(own1, own_half, 1, outputs)
    outputs = place(swap(send0, XL), 1 - own_half, 0, outputs)
    outputs = place(swap(send1, XL), 1 - own_half, 1, outputs)
    rotated, scales = last(came2.reshape(128, BLOCKS, 128), lo2, 2, *outputs)
    return rotated, scales.transpose(0, 1, 3, 2)


def solution(mesh):
    fine = Mesh(np.asarray(mesh.devices).reshape(SIZES), AXES)
    row, col = (XH, Y, Z), (XL, CORE)
    return jax.shard_map(
        local,
        mesh=fine,
        in_specs=(P(None, row, col), P(), P(), P(), P()),
        out_specs=(P(None, row, None, col), P(None, row, None, col)),
        check_vma=False,
    )
```

time: 204 us -> 181 us (0.89)
  starting transfers between devices: 49.1 us -> 36.6 us
  waiting for transfers between devices: 104 us -> 94.5 us
    all_to_all x3 -> x2, waiting for transfers between devices: 41.1 us -> 0.01 us  [the longest x1 0.01 us: local(): came2 = lax.all_to_all(sent2, (Y, Z), 0, 0, tiled=True)]
    ppermute x0 -> x3, waiting for transfers between devices: none -> 31.8 us  [local(): lax.ppermute(planes[d], (XH, XL), [(i, i ^ d) for i in range(4)])]
    all_to_all x3 -> x2, starting transfers between devices: 40.1 us -> 26.7 us  [the longest x1 16.8 us: local(): came01 = lax.all_to_all(sent01, (XH, Y, Z, XL), 0, 0, tiled=True)]
    pallas_call x1 -> x4, Pallas kernels: 4.3 us -> 11.2 us  [place(): pl.pallas_call(place_kernel, grid_spec=pltpu.PrefetchScalarGridSpec(num_s...]
    pallas_call x2 -> x1, Pallas kernels: 7.75 us -> 1.94 us  [right(): pl.pallas_call(right_kernel, in_specs=[WHOLE] * 5 + [ORDER] * len(after),...]
    pallas_call x2 -> x1, Pallas kernels: 9.28 us -> 3.78 us  [last(): pl.pallas_call(last_kernel, grid=(WIDTH // tile,), in_specs=[pl.BlockSpec...]
    ppermute x0 -> x3, starting transfers between devices: none -> 4.13 us  [local(): lax.ppermute(planes[d], (XH, XL), [(i, i ^ d) for i in range(4)])]
    pallas_call x4 -> x5, Pallas kernels: 20.1 us -> 23.6 us  [the longest x2 13.5 us: inner(): pl.pallas_call(functools.partial(inner_kernel, matrices, len(shapes)), in...]
  transfers between devices with their start and end apart: 11 -> 11, of which waited for: 4 -> 7; matrix products, arithmetic and copies ran while one was open for 1% -> 1% of each run, Pallas kernels for 16% -> 16%
where the time goes in v1:
time: 181 us
  waiting for transfers between devices  94.5 us (52%)
  Pallas kernels  40.6 us (22%)
  starting transfers between devices  36.6 us (20%)
  local copies, waits for them, and re-layouts  7.09 us (4%)
    ppermute x6, waiting for transfers between devices, swap(): return lax.ppermute(x, axis, [(0, 1), (1, 0)])  62.7 us
    ppermute x3, waiting for transfers between devices, local(): lax.ppermute(planes[d], (XH, XL), [(i, i ^ d) for i in range(4)])  31.8 us
    all_to_all x1, starting transfers between devices, local(): came01 = lax.all_to_all(sent01, (XH, Y, Z, XL), 0, 0, tiled=True)  16.8 us
    pallas_call x2, Pallas kernels, inner(): pl.pallas_call(functools.partial(inner_kernel, matrices, len(shapes)), in...  13.5 us
    pallas_call x4, Pallas kernels, place(): pl.pallas_call(place_kernel, grid_spec=pltpu.PrefetchScalarGridSpec(num_s...  11.2 us
    all_to_all x1, starting transfers between devices, local(): came2 = lax.all_to_all(sent2, (Y, Z), 0, 0, tiled=True)  9.91 us
    pallas_call x2, Pallas kernels, both(): pl.pallas_call(functools.partial(both_kernel, matrix), grid=(1,), in_spec...  8.79 us
    ppermute x6, starting transfers between devices, swap(): return lax.ppermute(x, axis, [(0, 1), (1, 0)])  5.78 us
  transfers between devices with their start and end apart: 11, of which 7 were waited for; matrix products, arithmetic and copies ran while one was open for 1% of the time, Pallas kernels for 16%

profile of v1, /device:TPU:1, one launch (start us, length us, event | category | flops | bytes accessed | tf_op | source)
XLA Modules:
  0.0 180.7 jit_solution(16414987444739388369)
XLA Ops:
  0.6 0.6 pad_add_fusion.place_ref
  1.3 8.0 %inner0.1.refs_0_ = bf16[128,2,56,128]{3,2,1,0:T(8,128)(2,1)} custom-call(s32[2]{0:T(128)} %pad_add_fusion.place_ref, bf16[3,128,7168]{2,1,0:T(8,128)(2,1)} %w_ref.3, bf16[128,128]{1,0:T(8,128)(2,1)} %li_ref.3, bf16[128,128]{1,0:T(8,128)(2,1)} %ri_ref.3), custom_call_target="tpu_custom_call" | custom-call | flops 469762048 | bytes 3670016 | tf_op jit(solution)/shard_map/inner0/pallas_call | solution.py:114
  9.2 16.8 %all-to-all-start.1 = ((bf16[128,2,56,128]{3,2,1,0:T(8,128)(2,1)}), bf16[128,2,56,128]{3,2,1,0:T(8,128)(2,1)}, u32[]{:S(2)}, u32[]{:S(2)}) async-start(bf16[128,2,56,128]{3,2,1,0:T(8,128)(2,1)} %inner0.1.refs_0_), calls=%async_computation.1 | async-start | bytes 7340032 | tf_op jit(solution)/shard_map/all_to_all | solution.py:396
  26.1 5.5 %inner2.1 = (bf16[64,56,128]{2,1,0:T(8,128)(2,1)}, bf16[64,56,128]{2,1,0:T(8,128)(2,1)}) custom-call(s32[2]{0:T(128)} %pad_add_fusion.place_ref, bf16[3,128,7168]{2,1,0:T(8,128)(2,1)} %w_ref.3, bf16[128,128]{1,0:T(8,128)(2,1)} %li_ref.3, bf16[128,128]{1,0:T(8,128)(2,1)} %ri_ref.3, bf16[128,2,56,128]{3,2,1,0:T(8,128)(2,1)} %inner0.1.refs_0_), custom_call_target="tpu_custom_call" | custom-call | flops 469762048 | bytes 3670016 | tf_op jit(solution)/shard_map/inner2/pallas_call | solution.py:114
  32.2 35.1 %collective-permute-done.refs_1_ = bf16[64,56,128]{2,1,0:T(8,128)(2,1)S(1)} collective-permute-done((bf16[64,56,128]{2,1,0:T(8,128)(2,1)}, bf16[64,56,128]{2,1,0:T(8,128)(2,1)S(1)}, u32[]{:S(2)}, u32[]{:S(2)}) %collective-permute-start) | collective-permute-done | bytes 917536 | tf_op jit(solution)/shard_map/ppermute | solution.py:373
  67.3 1.0 copy-done
  68.2 2.7 %collective-permute-start.1 = (bf16[64,56,128]{2,1,0:T(8,128)(2,1)}, bf16[64,56,128]{2,1,0:T(8,128)(2,1)S(1)}, u32[]{:S(2)}, u32[]{:S(2)}) collective-permute-start(bf16[64,56,128]{2,1,0:T(8,128)(2,1)} %gate.2.refs_0_), channel_id=1, source_target_pairs={{0,1},{1,0},{2,3},{3,2},{4,5},{5,4},{6,7},{7,6},{8,9},{9,8},{10,11... | collective-permute-start | bytes 2752520 | tf_op jit(solution)/shard_map/ppermute | solution.py:373
  71.4 0.6 rev.18
  72.4 0.8 collective-permute-done.1.refs_2_
  73.2 1.3 collective-permute-done.2.refs_3_
  74.5 1.2 copy-done.1
  75.7 1.2 copy-done.4
  76.9 1.9 %right.1 = (bf16[32,56,128]{2,1,0:T(8,128)(2,1)S(1)}, bf16[32,56,128]{2,1,0:T(8,128)(2,1)S(1)}, bf16[32,56,128]{2,1,0:T(8,128)(2,1)S(1)}, bf16[32,56,128]{2,1,0:T(8,128)(2,1)S(1)}) custom-call(bf16[112,224]{1,0:T(8,128)(2,1)S(1)} %reshape.31.ro_ref, bf16[64,56,128]{2,1,0:T(8,128)(2,1)S(1)} %copy-done.4, bf16[64,56,128]{2,1,0:T(8,128)(2,1)S(1)} %copy-done.1, ...), custom_call_target="tpu_custom_call" | custom-call | flops 23060000768 | bytes 5505024 | tf_op jit(solution)/shard_map/right/pallas_call | solution.py:166
  78.8 1.1 collective-permute-start.3
  80.0 2.8 %collective-permute-start.4 = (bf16[32,56,128]{2,1,0:T(8,128)(2,1)S(1)}, bf16[32,56,128]{2,1,0:T(8,128)(2,1)S(1)}, u32[]{:S(2)}, u32[]{:S(2)}) collective-permute-start(bf16[32,56,128]{2,1,0:T(8,128)(2,1)S(1)} %get-tuple-element.26), channel_id=1, source_target_pairs={{0,128},{2,130},{128,0},{130,2},{1,129},{3,131},{129,1},{131,3},{4... | collective-permute-start | bytes 1376264 | tf_op jit(solution)/shard_map/ppermute | solution.py:405
  82.9 16.0 %collective-permute-done.3.refs_1_ = bf16[32,56,128]{2,1,0:T(8,128)(2,1)S(1)} collective-permute-done((bf16[32,56,128]{2,1,0:T(8,128)(2,1)S(1)}, bf16[32,56,128]{2,1,0:T(8,128)(2,1)S(1)}, u32[]{:S(2)}, u32[]{:S(2)}) %collective-permute-start.3) | collective-permute-done | bytes 458784 | tf_op jit(solution)/shard_map/ppermute | solution.py:405
  99.0 15.8 %collective-permute-done.4.refs_2_ = bf16[32,56,128]{2,1,0:T(8,128)(2,1)S(1)} collective-permute-done((bf16[32,56,128]{2,1,0:T(8,128)(2,1)S(1)}, bf16[32,56,128]{2,1,0:T(8,128)(2,1)S(1)}, u32[]{:S(2)}, u32[]{:S(2)}) %collective-permute-start.4) | collective-permute-done | bytes 458784 | tf_op jit(solution)/shard_map/ppermute | solution.py:405
  114.8 1.4 join.1.refs_1_
  116.2 1.1 collective-permute-start.6
  117.3 9.9 %all-to-all-start = ((bf16[32,4,56,128]{3,2,1,0:T(8,128)(2,1)}), bf16[32,4,56,128]{3,2,1,0:T(8,128)(2,1)S(1)}, u32[]{:S(2)}, u32[]{:S(2)}) async-start(bf16[32,4,56,128]{3,2,1,0:T(8,128)(2,1)} %join.1.refs_1_), calls=%async_computation | async-start | bytes 3670016 | tf_op jit(solution)/shard_map/all_to_all | solution.py:410
  127.3 4.4 %both0.1 = (bf16[64,7168]{1,0:T(8,128)(2,1)S(1)}, bf16[64,7168]{1,0:T(8,128)(2,1)}) custom-call(bf16[112,224]{1,0:T(8,128)(2,1)S(1)} %reshape.33.ro_ref, bf16[64,64]{1,0:T(8,128)(2,1)S(1)} %copy-done.5, bf16[128,2,56,128]{3,2,1,0:T(8,128)(2,1)} %gate.3.own_ref, bf16[128,2,56,128]{3,2,1,0:T(8,128)(2,1)} %collective-permute-done.6.other_ref), custom_call_target="tpu_custom_call" | custom-call | flops 256901120 | bytes 5505024 | tf_op jit(solution)/shard_map/both0/pallas_call | solution.py:244
  132.1 4.4 %both1.1 = (bf16[64,7168]{1,0:T(8,128)(2,1)S(1)}, bf16[64,7168]{1,0:T(8,128)(2,1)}) custom-call(bf16[112,224]{1,0:T(8,128)(2,1)S(1)} %reshape.33.ro_ref, bf16[64,64]{1,0:T(8,128)(2,1)S(1)} %copy-done.5, bf16[128,2,56,128]{3,2,1,0:T(8,128)(2,1)} %gate.3.own_ref, bf16[128,2,56,128]{3,2,1,0:T(8,128)(2,1)} %collective-permute-done.6.other_ref), custom_call_target="tpu_custom_call" | custom-call | flops 256901120 | bytes 5505024 | tf_op jit(solution)/shard_map/both1/pallas_call | solution.py:244
  136.5 0.9 copy-done.2
  137.4 1.1 collective-permute-start.7
  139.1 2.0 %place0.2 = (bf16[3,2,64,7168]{3,2,1,0:T(8,128)(2,1)}, f32[3,2,56,64]{3,2,1,0:T(8,128)}) custom-call(s32[1]{0:T(128)} %bitcast.6.half_ref, bf16[64,7168]{1,0:T(8,128)(2,1)S(1)} %get-tuple-element.31.x_ref), custom_call_target="tpu_custom_call" | custom-call | flops 458752 | bytes 1835008 | tf_op jit(solution)/shard_map/place0/pallas_call | solution.py:339
  141.1 1.2 copy-done.3
  142.3 2.0 %place1.2 = (bf16[3,2,64,7168]{3,2,1,0:T(8,128)(2,1)}, f32[3,2,56,64]{3,2,1,0:T(8,128)}) custom-call(s32[1]{0:T(128)} %bitcast.6.half_ref, bf16[64,7168]{1,0:T(8,128)(2,1)S(1)} %copy-done.3, bf16[3,2,64,7168]{3,2,1,0:T(8,128)(2,1)} %get-tuple-element.32.refs_0_, f32[3,2,56,64]{3,2,1,0:T(8,128)} %get-tuple-element.33.refs_1_), custom_call_target="tpu_custom_call", output_to_operand_aliasing={{0}: (2, {}), {1}: (3, {})} | custom-call | flops 458752 | bytes 1835008 | tf_op jit(solution)/shard_map/place1/pallas_call | solution.py:339
  144.3 9.3 %collective-permute-done.8.x_ref = bf16[64,7168]{1,0:T(8,128)(2,1)} collective-permute-done((bf16[64,7168]{1,0:T(8,128)(2,1)}, bf16[64,7168]{1,0:T(8,128)(2,1)}, u32[]{:S(2)}, u32[]{:S(2)}) %collective-permute-start.8) | collective-permute-done | bytes 917536 | tf_op jit(solution)/shard_map/ppermute | solution.py:373
  153.7 3.6 %place0.3 = (bf16[3,2,64,7168]{3,2,1,0:T(8,128)(2,1)}, f32[3,2,56,64]{3,2,1,0:T(8,128)}) custom-call(s32[1]{0:T(128)S(6)} %sub.4.half_ref, bf16[64,7168]{1,0:T(8,128)(2,1)} %collective-permute-done.8.x_ref, bf16[3,2,64,7168]{3,2,1,0:T(8,128)(2,1)} %get-tuple-element.34.refs_0_, ...), custom_call_target="tpu_custom_call", output_to_operand_aliasing={{0}: (2, {}), {1}: (3, {})} | custom-call | flops 458752 | bytes 1835008 | tf_op jit(solution)/shard_map/place0/pallas_call | solution.py:339
  157.2 16.1 %collective-permute-done.7.x_ref = bf16[64,7168]{1,0:T(8,128)(2,1)} collective-permute-done((bf16[64,7168]{1,0:T(8,128)(2,1)}, bf16[64,7168]{1,0:T(8,128)(2,1)}, u32[]{:S(2)}, u32[]{:S(2)}) %collective-permute-start.7) | collective-permute-done | bytes 917536 | tf_op jit(solution)/shard_map/ppermute | solution.py:373
  173.3 3.6 %place1.3 = (bf16[3,2,64,7168]{3,2,1,0:T(8,128)(2,1)}, f32[3,2,56,64]{3,2,1,0:T(8,128)}) custom-call(s32[1]{0:T(128)S(6)} %sub.4.half_ref, bf16[64,7168]{1,0:T(8,128)(2,1)} %collective-permute-done.7.x_ref, bf16[3,2,64,7168]{3,2,1,0:T(8,128)(2,1)} %get-tuple-element.36.refs_0_, ...), custom_call_target="tpu_custom_call", output_to_operand_aliasing={{0}: (2, {}), {1}: (3, {})} | custom-call | flops 458752 | bytes 1835008 | tf_op jit(solution)/shard_map/place1/pallas_call | solution.py:339
  176.9 3.8 %last2.1 = (bf16[3,2,64,7168]{3,2,1,0:T(8,128)(2,1)}, f32[3,2,56,64]{3,2,1,0:T(8,128)}) custom-call(bf16[128,128]{1,0:T(8,128)(2,1)S(1)} %copy.24.lo_ref, bf16[128,56,128]{2,1,0:T(8,128)(2,1)S(1)} %bitcast.13, bf16[3,2,64,7168]{3,2,1,0:T(8,128)(2,1)} %get-tuple-element.38.refs_0_, ...), custom_call_target="tpu_custom_call", output_to_operand_aliasing={{0}: (2, {}), {1}: (3, {})} | custom-call | flops 234881024 | bytes 3670016 | tf_op jit(solution)/shard_map/last2/pallas_call | solution.py:302
  (35 shorter events, 2.7 us)
Async XLA Ops:
  9.2 107.0 %all-to-all-start.1 = ((bf16[128,2,56,128]{3,2,1,0:T(8,128)(2,1)}), bf16[128,2,56,128]{3,2,1,0:T(8,128)(2,1)}, u32[]{:S(2)}, u32[]{:S(2)}) async-start(bf16[128,2,56,128]{3,2,1,0:T(8,128)(2,1)} %inner0.1.refs_0_), calls=%async_computation.1 | async-start | bytes 7340032 | tf_op jit(solution)/shard_map/all_to_all | solution.py:396
  26.0 44.8 %copy-start.6 = (bf16[224,224]{1,0:T(8,128)(2,1)S(1)}, bf16[224,224]{1,0:T(8,128)(2,1)}, u32[]{:S(2)}) copy-start(bf16[224,224]{1,0:T(8,128)(2,1)} %param.8) | copy-start | bytes 301060
  31.6 35.7 %collective-permute-start = (bf16[64,56,128]{2,1,0:T(8,128)(2,1)}, bf16[64,56,128]{2,1,0:T(8,128)(2,1)S(1)}, u32[]{:S(2)}, u32[]{:S(2)}) collective-permute-start(bf16[64,56,128]{2,1,0:T(8,128)(2,1)} %get-tuple-element.23), channel_id=1, source_target_pairs={{0,2},{2,0},{1,3},{3,1},{4,6},{6,4},{5,7},{7,5},{8,10},{10,8},{9,1... | collective-permute-start | bytes 2752520 | tf_op jit(solution)/shard_map/ppermute | solution.py:373
  67.3 1.0 copy-start
  68.2 5.0 %collective-permute-start.1 = (bf16[64,56,128]{2,1,0:T(8,128)(2,1)}, bf16[64,56,128]{2,1,0:T(8,128)(2,1)S(1)}, u32[]{:S(2)}, u32[]{:S(2)}) collective-permute-start(bf16[64,56,128]{2,1,0:T(8,128)(2,1)} %gate.2.refs_0_), channel_id=1, source_target_pairs={{0,1},{1,0},{2,3},{3,2},{4,5},{5,4},{6,7},{7,6},{8,9},{9,8},{10,11... | collective-permute-start | bytes 2752520 | tf_op jit(solution)/shard_map/ppermute | solution.py:373
  70.9 3.6 %collective-permute-start.2 = (bf16[64,56,128]{2,1,0:T(8,128)(2,1)}, bf16[64,56,128]{2,1,0:T(8,128)(2,1)S(1)}, u32[]{:S(2)}, u32[]{:S(2)}) collective-permute-start(bf16[64,56,128]{2,1,0:T(8,128)(2,1)} %copy-done), channel_id=1, source_target_pairs={{0,1},{1,0},{2,3},{3,2},{4,5},{5,4},{6,7},{7,6},{8,9},{9,8},{10,11... | collective-permute-start | bytes 2752520 | tf_op jit(solution)/shard_map/ppermute | solution.py:373
  74.5 1.2 copy-start.1
  75.7 1.2 copy-start.4
  78.8 20.2 %collective-permute-start.3 = (bf16[32,56,128]{2,1,0:T(8,128)(2,1)S(1)}, bf16[32,56,128]{2,1,0:T(8,128)(2,1)S(1)}, u32[]{:S(2)}, u32[]{:S(2)}) collective-permute-start(bf16[32,56,128]{2,1,0:T(8,128)(2,1)S(1)} %get-tuple-element.25), channel_id=1, source_target_pairs={{0,2},{2,0},{128,130},{130,128},{1,3},{3,1},{129,131},{131,129},{4... | collective-permute-start | bytes 1376264 | tf_op jit(solution)/shard_map/ppermute | solution.py:405
  80.0 34.8 %collective-permute-start.4 = (bf16[32,56,128]{2,1,0:T(8,128)(2,1)S(1)}, bf16[32,56,128]{2,1,0:T(8,128)(2,1)S(1)}, u32[]{:S(2)}, u32[]{:S(2)}) collective-permute-start(bf16[32,56,128]{2,1,0:T(8,128)(2,1)S(1)} %get-tuple-element.26), channel_id=1, source_target_pairs={{0,128},{2,130},{128,0},{130,2},{1,129},{3,131},{129,1},{131,3},{4... | collective-permute-start | bytes 1376264 | tf_op jit(solution)/shard_map/ppermute | solution.py:405
  82.7 32.0 %collective-permute-start.5 = (bf16[32,56,128]{2,1,0:T(8,128)(2,1)S(1)}, bf16[32,56,128]{2,1,0:T(8,128)(2,1)S(1)}, u32[]{:S(2)}, u32[]{:S(2)}) collective-permute-start(bf16[32,56,128]{2,1,0:T(8,128)(2,1)S(1)} %get-tuple-element.27), channel_id=1, source_target_pairs={{0,130},{2,128},{128,2},{130,0},{1,131},{3,129},{129,3},{131,1},{4... | collective-permute-start | bytes 1376264 | tf_op jit(solution)/shard_map/ppermute | solution.py:405
  116.2 11.1 %copy-start.5 = (bf16[64,64]{1,0:T(8,128)(2,1)S(1)}, bf16[64,64]{1,0:T(8,128)(2,1)}, u32[]{:S(2)}) copy-start(bf16[64,64]{1,0:T(8,128)(2,1)} %lo_ref.3) | copy-start | bytes 24580
  116.2 11.1 %collective-permute-start.6 = (bf16[128,2,56,128]{3,2,1,0:T(8,128)(2,1)}, bf16[128,2,56,128]{3,2,1,0:T(8,128)(2,1)}, u32[]{:S(2)}, u32[]{:S(2)}) collective-permute-start(bf16[128,2,56,128]{3,2,1,0:T(8,128)(2,1)} %gate.3.own_ref), channel_id=1, source_target_pairs={{0,1},{1,0},{2,3},{3,2},{4,5},{5,4},{6,7},{7,6},{8,9},{9,8},{10,11... | collective-permute-start | bytes 11010056 | tf_op jit(solution)/shard_map/ppermute | solution.py:373
  117.3 59.7 %all-to-all-start = ((bf16[32,4,56,128]{3,2,1,0:T(8,128)(2,1)}), bf16[32,4,56,128]{3,2,1,0:T(8,128)(2,1)S(1)}, u32[]{:S(2)}, u32[]{:S(2)}) async-start(bf16[32,4,56,128]{3,2,1,0:T(8,128)(2,1)} %join.1.refs_1_), calls=%async_computation | async-start | bytes 3670016 | tf_op jit(solution)/shard_map/all_to_all | solution.py:410
  131.7 21.9 %collective-permute-start.8 = (bf16[64,7168]{1,0:T(8,128)(2,1)}, bf16[64,7168]{1,0:T(8,128)(2,1)}, u32[]{:S(2)}, u32[]{:S(2)}) collective-permute-start(bf16[64,7168]{1,0:T(8,128)(2,1)} %get-tuple-element.29), channel_id=1, source_target_pairs={{0,2},{2,0},{1,3},{3,1},{4,6},{6,4},{5,7},{7,5},{8,10},{10,8},{9,1... | collective-permute-start | bytes 2752520 | tf_op jit(solution)/shard_map/ppermute | solution.py:373
  136.5 0.9 copy-start.2
  137.4 35.9 %collective-permute-start.7 = (bf16[64,7168]{1,0:T(8,128)(2,1)}, bf16[64,7168]{1,0:T(8,128)(2,1)}, u32[]{:S(2)}, u32[]{:S(2)}) collective-permute-start(bf16[64,7168]{1,0:T(8,128)(2,1)} %get-tuple-element.28), channel_id=1, source_target_pairs={{0,2},{2,0},{1,3},{3,1},{4,6},{6,4},{5,7},{7,5},{8,10},{10,8},{9,1... | collective-permute-start | bytes 2752520 | tf_op jit(solution)/shard_map/ppermute | solution.py:373
  141.1 1.2 copy-start.3

commit v2 on v1

--- a/solution.py
+++ b/solution.py
@@ -16,9 +16,11 @@
 SIZES = (2, 4, 8, 2, 2)
 WIDTH = 7168
 BLOCKS = 56
-VMEM = 24 * 1024 * 1024
-INNER_VMEM = 60 * 1024 * 1024
+MIB = 1024 * 1024
+VMEM = 24 * MIB
+INNER_VMEM = 60 * MIB
 MICROS = 20
+PITCH = BLOCKS + 1
 WHOLE = pl.BlockSpec(memory_space=pltpu.VMEM)
 ORDER = pl.BlockSpec(memory_space=pl.ANY)
 
@@ -79,7 +81,7 @@
             )
             second = matmul(li, first)
             for p in range(tile // 128):
-                turned[pl.ds(t * (tile // 128) + p, 128, stride=BLOCKS), :] = second[
+                turned[pl.ds(t * (tile // 128) + p, 128, stride=PITCH), :] = second[
                     :, p * 128 : (p + 1) * 128
                 ]
         for part in range(4):
@@ -87,11 +89,11 @@
             for r in range(32):
                 if outs == 1:
                     to = part * 32 + r
-                    row = to * BLOCKS
+                    row = to * PITCH
                 else:
                     to = half * 64 + part % 2 * 32 + r
                     at = (place_ref[0] ^ (part % 2)) * 32 + r
-                    row = pl.multiple_of((2 * at + (place_ref[1] ^ half)) * BLOCKS, 8)
+                    row = (2 * at + (place_ref[1] ^ half)) * PITCH
                 packed[place, to] = turned[pl.ds(row, BLOCKS), :].astype(BF16)
             if outs == 1:
                 here, there = part * 32, o_refs[0].at[pl.ds(part * 32, 32), place]
@@ -119,7 +121,7 @@
         out_shape=shapes,
         scratch_shapes=[
             pltpu.VMEM((4 * count, 128, WIDTH // 4), BF16),
-            pltpu.VMEM((128 * BLOCKS, 128), F32),
+            pltpu.VMEM((128 * PITCH, 128), F32),
             pltpu.VMEM((count, 128, BLOCKS, 128), BF16),
             pltpu.SemaphoreType.DMA((4 * count,)),
             pltpu.SemaphoreType.DMA((4 * count,)),
@@ -211,14 +213,30 @@
 
 
 def both_kernel(matrix, ro_ref, lo_ref, own_ref, other_ref, *refs):
-    o_refs, turned = refs[-3:-1], refs[-1]
+    o_refs, (held, turned, sems) = refs[-5:-3], refs[-3:]
+    arriving = [
+        [
+            pltpu.make_async_copy(
+                ref.at[pl.ds(part * 32, 32), matrix],
+                held.at[at, pl.ds(part * 32, 32)],
+                sems.at[at, part],
+            )
+            for at, ref in enumerate((own_ref, other_ref))
+        ]
+        for part in range(4)
+    ]
+    for part in arriving:
+        for copy in part:
+            copy.start()
     ro = ro_ref[...]
-    sources = (own_ref, own_ref, other_ref, other_ref)
-    stride = 72
+    stride = 73
     for first in range(0, 64, 4):
+        if first % 16 == 0:
+            for copy in arriving[first // 16]:
+                copy.wait()
         rows = range(first, first + 4)
-        where = [((2 * r, 0), (2 * r + 1, 0)) * 2 for r in rows]
-        mixed = mix_blocks(sources, where, ro)
+        where = [[(at, 2 * r + half) for at in (0, 1) for half in (0, 1)] for r in rows]
+        mixed = mix_blocks([held] * 4, where, ro)
         for at, r in enumerate(rows):
             turned[pl.ds(r, 2 * BLOCKS, stride=stride), :] = mixed[
                 :, at * 128 : at * 128 + 128
@@ -239,16 +257,18 @@
 
 
 def both(own, other, matrix, ro, lo):
-    fixed = lambda shape: pl.BlockSpec(shape, lambda i: (0,) * len(shape))
-    blocks = pl.BlockSpec((128, 1, BLOCKS, 128), lambda i: (0, matrix, 0, 0))
+    hbm = pl.BlockSpec(memory_space=pltpu.HBM)
     return pl.pallas_call(
         functools.partial(both_kernel, matrix),
-        grid=(1,),
-        in_specs=[fixed(ro.shape), fixed(lo.shape), blocks, blocks],
-        out_specs=[fixed((64, WIDTH))] * 2,
+        in_specs=[WHOLE, WHOLE, hbm, hbm],
+        out_specs=[WHOLE] * 2,
         out_shape=[jax.ShapeDtypeStruct((64, WIDTH), BF16)] * 2,
-        scratch_shapes=[pltpu.VMEM((2 * BLOCKS * 72, 128), F32)],
-        compiler_params=pltpu.CompilerParams(vmem_limit_bytes=VMEM),
+        scratch_shapes=[
+            pltpu.VMEM((2, 128, BLOCKS, 128), BF16),
+            pltpu.VMEM((2 * BLOCKS * 73, 128), F32),
+            pltpu.SemaphoreType.DMA((2, 4)),
+        ],
+        compiler_params=pltpu.CompilerParams(vmem_limit_bytes=18 * MIB),
         cost_estimate=cost(10 * 64 * BLOCKS * WIDTH, 3),
         name=f"both{matrix}",
     )(ro, lo, own, other)
@@ -273,7 +293,7 @@
     o_ref, s_ref, turned, held = refs[-4:]
     step = pl.program_id(0)
     tile = o_ref.shape[3]
-    stride = 136
+    stride = 137
 
     @pl.when(step == 0)
     def _():
@@ -283,7 +303,7 @@
     first = step * (tile // 128)
     x = jnp.concatenate(
         [
-            turned[pl.ds(pl.multiple_of((first + p) * stride, 8), 128), :].astype(BF16)
+            turned[pl.ds((first + p) * stride, 128), :].astype(BF16)
             for p in range(tile // 128)
         ],
         axis=1,
@@ -314,11 +334,11 @@
         ],
         out_shape=OUTPUTS,
         scratch_shapes=[
-            pltpu.VMEM((BLOCKS * 136, 128), F32),
+            pltpu.VMEM((BLOCKS * 137, 128), F32),
             pltpu.VMEM((128, 128), F32),
         ],
         input_output_aliases={2: 0, 3: 1},
-        compiler_params=pltpu.CompilerParams(vmem_limit_bytes=VMEM),
+        compiler_params=pltpu.CompilerParams(vmem_limit_bytes=12 * MIB),
         cost_estimate=cost(2 * 128 * 128 * WIDTH, 2),
         name=f"last{matrix}",
     )(lo, x, rotated, scales)
@@ -351,7 +371,7 @@
         ),
         out_shape=OUTPUTS,
         input_output_aliases={2: 0, 3: 1} if into else {},
-        compiler_params=pltpu.CompilerParams(vmem_limit_bytes=VMEM),
+        compiler_params=pltpu.CompilerParams(vmem_limit_bytes=6 * MIB),
         cost_estimate=cost(64 * WIDTH, 1),
         name=f"place{matrix}",
     )(half, x, *into)
@@ -392,14 +412,16 @@
     ro2 = jnp.where(xl == 0, ro, ro[::-1, :, :, ::-1]).reshape(2 * BLOCKS, 4 * BLOCKS)
 
     sent01_shape = jax.ShapeDtypeStruct((128, 2, BLOCKS, 128), BF16)
-    (sent01,) = inner(weights, (0, 1), where, left_inner, right_inner, [sent01_shape])
+    nowhere = jnp.zeros((2,), jnp.int32)
+    (sent01,) = inner(
+        weights, (0, 1), nowhere, left_inner, right_inner, [sent01_shape]
+    )
     came01 = lax.all_to_all(sent01, (XH, Y, Z, XL), 0, 0, tiled=True)
 
     keep2, send2 = inner(
         weights, (2,), where, left_inner, right_inner, [blocks_of(64)] * 2, [sent01]
     )
     came2 = swap(send2, XL)
-    keep2 = gate(keep2, [came2])
     planes = right([keep2, came2, swap(keep2, CORE), swap(came2, CORE)], ro2)
     planes = [planes[0]] + [
         lax.ppermute(planes[d], (XH, XL), [(i, i ^ d) for i in range(4)])
@@ -415,8 +437,8 @@
     outputs = place(own0, own_half, 0)
     outputs = place(own1, own_half, 1, outputs)
     outputs = place(swap(send0, XL), 1 - own_half, 0, outputs)
-    outputs = place(swap(send1, XL), 1 - own_half, 1, outputs)
-    rotated, scales = last(came2.reshape(128, BLOCKS, 128), lo2, 2, *outputs)
+    outputs = last(came2.reshape(128, BLOCKS, 128), lo2, 2, *outputs)
+    rotated, scales = place(swap(send1, XL), 1 - own_half, 1, outputs)
     return rotated, scales.transpose(0, 1, 3, 2)
 
 

time: 181 us -> 176 us (0.972)
  waiting for transfers between devices: 94.5 us -> 91.2 us
    ppermute x6, waiting for transfers between devices: 62.7 us -> 44.2 us  [swap(): return lax.ppermute(x, axis, [(0, 1), (1, 0)])]
    all_to_all x1, waiting for transfers between devices: 0.01 us -> 14 us  [local(): came2 = lax.all_to_all(sent2, (Y, Z), 0, 0, tiled=True)]
    unnamed x16 -> x12, local copies, waits for them, and re-layouts: 5.6 us -> 3.46 us
  transfers between devices with their start and end apart: 11 -> 11, of which waited for: 7 -> 6; matrix products, arithmetic and copies ran while one was open for 1% -> 2% of each run, Pallas kernels for 16% -> 16%
where the time goes in v2:
time: 176 us; the launch traced here: 175 us
  waiting for transfers between devices  91.2 us (52%)
  Pallas kernels  38.9 us (22%)
  starting transfers between devices  37.8 us (21%)
  local copies, waits for them, and re-layouts  5.46 us (3%)
    ppermute x6, waiting for transfers between devices, swap(): return lax.ppermute(x, axis, [(0, 1), (1, 0)])  44.2 us
    ppermute x3, waiting for transfers between devices, local(): lax.ppermute(planes[d], (XH, XL), [(i, i ^ d) for i in range(4)])  32.9 us
    all_to_all x1, starting transfers between devices, local(): came01 = lax.all_to_all(sent01, (XH, Y, Z, XL), 0, 0, tiled=True)  16.8 us
    all_to_all x1, waiting for transfers between devices, local(): came2 = lax.all_to_all(sent2, (Y, Z), 0, 0, tiled=True)  14 us
    pallas_call x2, Pallas kernels, inner(): pl.pallas_call(functools.partial(inner_kernel, matrices, len(shapes)), in...  13.3 us
    pallas_call x4, Pallas kernels, place(): pl.pallas_call(place_kernel, grid_spec=pltpu.PrefetchScalarGridSpec(num_s...  11.2 us
    all_to_all x1, starting transfers between devices, local(): came2 = lax.all_to_all(sent2, (Y, Z), 0, 0, tiled=True)  9.83 us
    pallas_call x2, Pallas kernels, both(): pl.pallas_call(functools.partial(both_kernel, matrix), in_specs=[WHOLE, W...  7.81 us
  transfers between devices with their start and end apart: 11, of which 6 were waited for; matrix products, arithmetic and copies ran while one was open for 2% of the time, Pallas kernels for 16%

profile of v2, /device:TPU:1, one launch (start us, length us, event | category | flops | bytes accessed | tf_op | source)
XLA Modules:
  0.0 175.3 jit_solution(18391168519516979682)
XLA Ops:
  0.6 0.5 broadcast_1_place_ref.2.place_ref
  1.1 7.9 %inner0.1.refs_0_ = bf16[128,2,56,128]{3,2,1,0:T(8,128)(2,1)} custom-call(s32[2]{0:T(128)} %broadcast_1_place_ref.2.place_ref, bf16[3,128,7168]{2,1,0:T(8,128)(2,1)} %w_ref.3, bf16[128,128]{1,0:T(8,128)(2,1)} %li_ref.3, bf16[128,128]{1,0:T(8,128)(2,1)} %ri_ref.3), custom_call_target="tpu_custom_call" | custom-call | flops 469762048 | bytes 3670016 | tf_op jit(solution)/shard_map/inner0/pallas_call | solution.py:116
  9.0 16.8 %all-to-all-start = ((bf16[128,2,56,128]{3,2,1,0:T(8,128)(2,1)}), bf16[128,2,56,128]{3,2,1,0:T(8,128)(2,1)}, u32[]{:S(2)}, u32[]{:S(2)}) async-start(bf16[128,2,56,128]{3,2,1,0:T(8,128)(2,1)} %inner0.1.refs_0_), calls=%async_computation | async-start | bytes 7340032 | tf_op jit(solution)/shard_map/all_to_all | solution.py:419
  25.9 0.6 pad_add_fusion.place_ref
  26.5 5.4 %inner2.1 = (bf16[64,56,128]{2,1,0:T(8,128)(2,1)}, bf16[64,56,128]{2,1,0:T(8,128)(2,1)}) custom-call(s32[2]{0:T(128)} %pad_add_fusion.place_ref, bf16[3,128,7168]{2,1,0:T(8,128)(2,1)} %w_ref.3, bf16[128,128]{1,0:T(8,128)(2,1)} %li_ref.3, bf16[128,128]{1,0:T(8,128)(2,1)} %ri_ref.3, bf16[128,2,56,128]{3,2,1,0:T(8,128)(2,1)} %inner0.1.refs_0_), custom_call_target="tpu_custom_call" | custom-call | flops 469762048 | bytes 3670016 | tf_op jit(solution)/shard_map/inner2/pallas_call | solution.py:116
  31.9 0.6 collective-permute-start
  32.5 1.5 collective-permute-start.1
  34.0 33.8 %collective-permute-done.refs_1_ = bf16[64,56,128]{2,1,0:T(8,128)(2,1)S(1)} collective-permute-done((bf16[64,56,128]{2,1,0:T(8,128)(2,1)}, bf16[64,56,128]{2,1,0:T(8,128)(2,1)S(1)}, u32[]{:S(2)}, u32[]{:S(2)}) %collective-permute-start) | collective-permute-done | bytes 917536 | tf_op jit(solution)/shard_map/ppermute | solution.py:393
  67.8 2.3 %collective-permute-start.2 = (bf16[64,56,128]{2,1,0:T(8,128)(2,1)S(1)}, bf16[64,56,128]{2,1,0:T(8,128)(2,1)S(1)}, u32[]{:S(2)}, u32[]{:S(2)}) collective-permute-start(bf16[64,56,128]{2,1,0:T(8,128)(2,1)S(1)} %collective-permute-done.refs_1_), channel_id=1, source_target_pairs={{0,1},{1,0},{2,3},{3,2},{4,5},{5,4},{6,7},{7,6},{8,9},{9,8},{10,11... | collective-permute-start | bytes 2752520 | tf_op jit(solution)/shard_map/ppermute | solution.py:393
  70.7 0.6 rev.17
  71.6 0.6 collective-permute-done.2.refs_3_
  72.2 1.2 copy-done.3
  73.4 1.9 %right.1 = (bf16[32,56,128]{2,1,0:T(8,128)(2,1)S(1)}, bf16[32,56,128]{2,1,0:T(8,128)(2,1)S(1)}, bf16[32,56,128]{2,1,0:T(8,128)(2,1)S(1)}, bf16[32,56,128]{2,1,0:T(8,128)(2,1)S(1)}) custom-call(bf16[112,224]{1,0:T(8,128)(2,1)S(1)} %reshape.31.ro_ref, bf16[64,56,128]{2,1,0:T(8,128)(2,1)S(1)} %copy-done.3, ...), custom_call_target="tpu_custom_call" | custom-call | flops 23060000768 | bytes 5505024 | tf_op jit(solution)/shard_map/right/pallas_call | solution.py:168
  75.4 0.8 collective-permute-start.3
  76.1 2.9 %collective-permute-start.4 = (bf16[32,56,128]{2,1,0:T(8,128)(2,1)S(1)}, bf16[32,56,128]{2,1,0:T(8,128)(2,1)S(1)}, u32[]{:S(2)}, u32[]{:S(2)}) collective-permute-start(bf16[32,56,128]{2,1,0:T(8,128)(2,1)S(1)} %get-tuple-element.26), channel_id=1, source_target_pairs={{0,128},{2,130},{128,0},{130,2},{1,129},{3,131},{129,1},{131,3},{4... | collective-permute-start | bytes 1376264 | tf_op jit(solution)/shard_map/ppermute | solution.py:427
  79.3 15.1 %collective-permute-done.3.refs_1_ = bf16[32,56,128]{2,1,0:T(8,128)(2,1)S(1)} collective-permute-done((bf16[32,56,128]{2,1,0:T(8,128)(2,1)S(1)}, bf16[32,56,128]{2,1,0:T(8,128)(2,1)S(1)}, u32[]{:S(2)}, u32[]{:S(2)}) %collective-permute-start.3) | collective-permute-done | bytes 458784 | tf_op jit(solution)/shard_map/ppermute | solution.py:427
  94.4 17.8 %collective-permute-done.4.refs_2_ = bf16[32,56,128]{2,1,0:T(8,128)(2,1)S(1)} collective-permute-done((bf16[32,56,128]{2,1,0:T(8,128)(2,1)S(1)}, bf16[32,56,128]{2,1,0:T(8,128)(2,1)S(1)}, u32[]{:S(2)}, u32[]{:S(2)}) %collective-permute-start.4) | collective-permute-done | bytes 458784 | tf_op jit(solution)/shard_map/ppermute | solution.py:427
  112.2 1.4 join.1.refs_1_
  113.7 1.3 collective-permute-start.6
  114.9 9.8 %all-to-all-start.1 = ((bf16[32,4,56,128]{3,2,1,0:T(8,128)(2,1)}), bf16[32,4,56,128]{3,2,1,0:T(8,128)(2,1)S(1)}, u32[]{:S(2)}, u32[]{:S(2)}) async-start(bf16[32,4,56,128]{3,2,1,0:T(8,128)(2,1)} %join.1.refs_1_), calls=%async_computation.1 | async-start | bytes 3670016 | tf_op jit(solution)/shard_map/all_to_all | solution.py:432
  124.9 3.9 %both0.1 = (bf16[64,7168]{1,0:T(8,128)(2,1)S(1)}, bf16[64,7168]{1,0:T(8,128)(2,1)}) custom-call(bf16[112,224]{1,0:T(8,128)(2,1)S(1)} %reshape.30.ro_ref, bf16[64,64]{1,0:T(8,128)(2,1)S(1)} %copy-done.2, bf16[128,2,56,128]{3,2,1,0:T(8,128)(2,1)} %gate.1.own_ref, bf16[128,2,56,128]{3,2,1,0:T(8,128)(2,1)} %collective-permute-done.6.other_ref), custom_call_target="tpu_custom_call" | custom-call | flops 256901120 | bytes 5505024 | tf_op jit(solution)/shard_map/both0/pallas_call | solution.py:261
  129.2 3.9 %both1.1 = (bf16[64,7168]{1,0:T(8,128)(2,1)S(1)}, bf16[64,7168]{1,0:T(8,128)(2,1)}) custom-call(bf16[112,224]{1,0:T(8,128)(2,1)S(1)} %reshape.30.ro_ref, bf16[64,64]{1,0:T(8,128)(2,1)S(1)} %copy-done.2, bf16[128,2,56,128]{3,2,1,0:T(8,128)(2,1)} %gate.1.own_ref, bf16[128,2,56,128]{3,2,1,0:T(8,128)(2,1)} %collective-permute-done.6.other_ref), custom_call_target="tpu_custom_call" | custom-call | flops 256901120 | bytes 5505024 | tf_op jit(solution)/shard_map/both1/pallas_call | solution.py:261
  133.2 0.9 copy-done
  134.1 1.1 collective-permute-start.7
  135.8 2.0 %place0.2 = (bf16[3,2,64,7168]{3,2,1,0:T(8,128)(2,1)}, f32[3,2,56,64]{3,2,1,0:T(8,128)}) custom-call(s32[1]{0:T(128)} %bitcast.half_ref, bf16[64,7168]{1,0:T(8,128)(2,1)S(1)} %get-tuple-element.31.x_ref), custom_call_target="tpu_custom_call" | custom-call | flops 458752 | bytes 1835008 | tf_op jit(solution)/shard_map/place0/pallas_call | solution.py:359
  137.8 1.2 copy-done.1
  139.0 2.0 %place1.2 = (bf16[3,2,64,7168]{3,2,1,0:T(8,128)(2,1)}, f32[3,2,56,64]{3,2,1,0:T(8,128)}) custom-call(s32[1]{0:T(128)} %bitcast.half_ref, bf16[64,7168]{1,0:T(8,128)(2,1)S(1)} %copy-done.1, bf16[3,2,64,7168]{3,2,1,0:T(8,128)(2,1)} %get-tuple-element.32.refs_0_, f32[3,2,56,64]{3,2,1,0:T(8,128)} %get-tuple-element.33.refs_1_), custom_call_target="tpu_custom_call", output_to_operand_aliasing={{0}: (2, {}), {1}: (3, {})} | custom-call | flops 458752 | bytes 1835008 | tf_op jit(solution)/shard_map/place1/pallas_call | solution.py:359
  141.0 9.8 %collective-permute-done.8.x_ref = bf16[64,7168]{1,0:T(8,128)(2,1)} collective-permute-done((bf16[64,7168]{1,0:T(8,128)(2,1)}, bf16[64,7168]{1,0:T(8,128)(2,1)}, u32[]{:S(2)}, u32[]{:S(2)}) %collective-permute-start.8) | collective-permute-done | bytes 917536 | tf_op jit(solution)/shard_map/ppermute | solution.py:393
  150.9 3.6 %place0.3 = (bf16[3,2,64,7168]{3,2,1,0:T(8,128)(2,1)}, f32[3,2,56,64]{3,2,1,0:T(8,128)}) custom-call(s32[1]{0:T(128)S(6)} %sub.4.half_ref, bf16[64,7168]{1,0:T(8,128)(2,1)} %collective-permute-done.8.x_ref, bf16[3,2,64,7168]{3,2,1,0:T(8,128)(2,1)} %get-tuple-element.34.refs_0_, ...), custom_call_target="tpu_custom_call", output_to_operand_aliasing={{0}: (2, {}), {1}: (3, {})} | custom-call | flops 458752 | bytes 1835008 | tf_op jit(solution)/shard_map/place0/pallas_call | solution.py:359
  154.5 14.0 %all-to-all-done.1 = bf16[32,4,56,128]{3,2,1,0:T(8,128)(2,1)S(1)} async-done(((bf16[32,4,56,128]{3,2,1,0:T(8,128)(2,1)}), bf16[32,4,56,128]{3,2,1,0:T(8,128)(2,1)S(1)}, u32[]{:S(2)}, u32[]{:S(2)}) %all-to-all-start.1) | async-done | bytes 1835040 | tf_op jit(solution)/shard_map/all_to_all | solution.py:432
  168.5 3.2 %last2.1 = (bf16[3,2,64,7168]{3,2,1,0:T(8,128)(2,1)}, f32[3,2,56,64]{3,2,1,0:T(8,128)}) custom-call(bf16[128,128]{1,0:T(8,128)(2,1)S(1)} %copy.23.lo_ref, bf16[128,56,128]{2,1,0:T(8,128)(2,1)S(1)} %bitcast.13, bf16[3,2,64,7168]{3,2,1,0:T(8,128)(2,1)} %get-tuple-element.36.refs_0_, ...), custom_call_target="tpu_custom_call", output_to_operand_aliasing={{0}: (2, {}), {1}: (3, {})} | custom-call | flops 234881024 | bytes 3670016 | tf_op jit(solution)/shard_map/last2/pallas_call | solution.py:322
  171.7 3.6 %place1.3 = (bf16[3,2,64,7168]{3,2,1,0:T(8,128)(2,1)}, f32[3,2,56,64]{3,2,1,0:T(8,128)}) custom-call(s32[1]{0:T(128)S(6)} %sub.4.half_ref, bf16[64,7168]{1,0:T(8,128)(2,1)} %collective-permute-done.7.x_ref, bf16[3,2,64,7168]{3,2,1,0:T(8,128)(2,1)} %get-tuple-element.38.refs_0_, ...), custom_call_target="tpu_custom_call", output_to_operand_aliasing={{0}: (2, {}), {1}: (3, {})} | custom-call | flops 458752 | bytes 1835008 | tf_op jit(solution)/shard_map/place1/pallas_call | solution.py:359
  (31 shorter events, 2.2 us)
Async XLA Ops:
  9.0 104.6 %all-to-all-start = ((bf16[128,2,56,128]{3,2,1,0:T(8,128)(2,1)}), bf16[128,2,56,128]{3,2,1,0:T(8,128)(2,1)}, u32[]{:S(2)}, u32[]{:S(2)}) async-start(bf16[128,2,56,128]{3,2,1,0:T(8,128)(2,1)} %inner0.1.refs_0_), calls=%async_computation | async-start | bytes 7340032 | tf_op jit(solution)/shard_map/all_to_all | solution.py:419
  25.9 44.3 %copy-start.4 = (bf16[224,224]{1,0:T(8,128)(2,1)S(1)}, bf16[224,224]{1,0:T(8,128)(2,1)}, u32[]{:S(2)}) copy-start(bf16[224,224]{1,0:T(8,128)(2,1)} %param.8) | copy-start | bytes 301060
  31.9 35.9 %collective-permute-start = (bf16[64,56,128]{2,1,0:T(8,128)(2,1)}, bf16[64,56,128]{2,1,0:T(8,128)(2,1)S(1)}, u32[]{:S(2)}, u32[]{:S(2)}) collective-permute-start(bf16[64,56,128]{2,1,0:T(8,128)(2,1)} %get-tuple-element.23), channel_id=1, source_target_pairs={{0,2},{2,0},{1,3},{3,1},{4,6},{6,4},{5,7},{7,5},{8,10},{10,8},{9,1... | collective-permute-start | bytes 2752520 | tf_op jit(solution)/shard_map/ppermute | solution.py:393
  32.5 39.1 %collective-permute-start.1 = (bf16[64,56,128]{2,1,0:T(8,128)(2,1)}, bf16[64,56,128]{2,1,0:T(8,128)(2,1)S(1)}, u32[]{:S(2)}, u32[]{:S(2)}) collective-permute-start(bf16[64,56,128]{2,1,0:T(8,128)(2,1)} %get-tuple-element.22.refs_0_), channel_id=1, source_target_pairs={{0,1},{1,0},{2,3},{3,2},{4,5},{5,4},{6,7},{7,6},{8,9},{9,8},{10,11... | collective-permute-start | bytes 2752520 | tf_op jit(solution)/shard_map/ppermute | solution.py:393
  67.8 4.4 %collective-permute-start.2 = (bf16[64,56,128]{2,1,0:T(8,128)(2,1)S(1)}, bf16[64,56,128]{2,1,0:T(8,128)(2,1)S(1)}, u32[]{:S(2)}, u32[]{:S(2)}) collective-permute-start(bf16[64,56,128]{2,1,0:T(8,128)(2,1)S(1)} %collective-permute-done.refs_1_), channel_id=1, source_target_pairs={{0,1},{1,0},{2,3},{3,2},{4,5},{5,4},{6,7},{7,6},{8,9},{9,8},{10,11... | collective-permute-start | bytes 2752520 | tf_op jit(solution)/shard_map/ppermute | solution.py:393
  72.2 1.2 copy-start.3
  75.4 19.1 %collective-permute-start.3 = (bf16[32,56,128]{2,1,0:T(8,128)(2,1)S(1)}, bf16[32,56,128]{2,1,0:T(8,128)(2,1)S(1)}, u32[]{:S(2)}, u32[]{:S(2)}) collective-permute-start(bf16[32,56,128]{2,1,0:T(8,128)(2,1)S(1)} %get-tuple-element.25), channel_id=1, source_target_pairs={{0,2},{2,0},{128,130},{130,128},{1,3},{3,1},{129,131},{131,129},{4... | collective-permute-start | bytes 1376264 | tf_op jit(solution)/shard_map/ppermute | solution.py:427
  76.1 36.1 %collective-permute-start.4 = (bf16[32,56,128]{2,1,0:T(8,128)(2,1)S(1)}, bf16[32,56,128]{2,1,0:T(8,128)(2,1)S(1)}, u32[]{:S(2)}, u32[]{:S(2)}) collective-permute-start(bf16[32,56,128]{2,1,0:T(8,128)(2,1)S(1)} %get-tuple-element.26), channel_id=1, source_target_pairs={{0,128},{2,130},{128,0},{130,2},{1,129},{3,131},{129,1},{131,3},{4... | collective-permute-start | bytes 1376264 | tf_op jit(solution)/shard_map/ppermute | solution.py:427
  79.1 33.2 %collective-permute-start.5 = (bf16[32,56,128]{2,1,0:T(8,128)(2,1)S(1)}, bf16[32,56,128]{2,1,0:T(8,128)(2,1)S(1)}, u32[]{:S(2)}, u32[]{:S(2)}) collective-permute-start(bf16[32,56,128]{2,1,0:T(8,128)(2,1)S(1)} %get-tuple-element.27), channel_id=1, source_target_pairs={{0,130},{2,128},{128,2},{130,0},{1,131},{3,129},{129,3},{131,1},{4... | collective-permute-start | bytes 1376264 | tf_op jit(solution)/shard_map/ppermute | solution.py:427
  113.6 11.3 %copy-start.2 = (bf16[64,64]{1,0:T(8,128)(2,1)S(1)}, bf16[64,64]{1,0:T(8,128)(2,1)}, u32[]{:S(2)}) copy-start(bf16[64,64]{1,0:T(8,128)(2,1)} %lo_ref.3) | copy-start | bytes 24580
  113.7 11.2 %collective-permute-start.6 = (bf16[128,2,56,128]{3,2,1,0:T(8,128)(2,1)}, bf16[128,2,56,128]{3,2,1,0:T(8,128)(2,1)}, u32[]{:S(2)}, u32[]{:S(2)}) collective-permute-start(bf16[128,2,56,128]{3,2,1,0:T(8,128)(2,1)} %gate.1.own_ref), channel_id=1, source_target_pairs={{0,1},{1,0},{2,3},{3,2},{4,5},{5,4},{6,7},{7,6},{8,9},{9,8},{10,11... | collective-permute-start | bytes 11010056 | tf_op jit(solution)/shard_map/ppermute | solution.py:393
  114.9 53.6 %all-to-all-start.1 = ((bf16[32,4,56,128]{3,2,1,0:T(8,128)(2,1)}), bf16[32,4,56,128]{3,2,1,0:T(8,128)(2,1)S(1)}, u32[]{:S(2)}, u32[]{:S(2)}) async-start(bf16[32,4,56,128]{3,2,1,0:T(8,128)(2,1)} %join.1.refs_1_), calls=%async_computation.1 | async-start | bytes 3670016 | tf_op jit(solution)/shard_map/all_to_all | solution.py:432
  128.8 22.1 %collective-permute-start.8 = (bf16[64,7168]{1,0:T(8,128)(2,1)}, bf16[64,7168]{1,0:T(8,128)(2,1)}, u32[]{:S(2)}, u32[]{:S(2)}) collective-permute-start(bf16[64,7168]{1,0:T(8,128)(2,1)} %get-tuple-element.29), channel_id=1, source_target_pairs={{0,2},{2,0},{1,3},{3,1},{4,6},{6,4},{5,7},{7,5},{8,10},{10,8},{9,1... | collective-permute-start | bytes 2752520 | tf_op jit(solution)/shard_map/ppermute | solution.py:393
  133.1 0.9 copy-start
  134.1 37.6 %collective-permute-start.7 = (bf16[64,7168]{1,0:T(8,128)(2,1)}, bf16[64,7168]{1,0:T(8,128)(2,1)}, u32[]{:S(2)}, u32[]{:S(2)}) collective-permute-start(bf16[64,7168]{1,0:T(8,128)(2,1)} %get-tuple-element.28), channel_id=1, source_target_pairs={{0,2},{2,0},{1,3},{3,1},{4,6},{6,4},{5,7},{7,5},{8,10},{10,8},{9,1... | collective-permute-start | bytes 2752520 | tf_op jit(solution)/shard_map/ppermute | solution.py:393
  137.8 1.2 copy-start.1

commit v3 on v2

--- a/solution.py
+++ b/solution.py
@@ -39,9 +39,12 @@
     )
 
 
-def inner_kernel(matrices, outs, place_ref, w_ref, li_ref, ri_ref, *refs):
+def inner_kernel(matrices, outs, *refs):
+    if outs == 2:
+        place_ref, refs = refs[0], refs[1:]
+    w_ref, li_ref, ri_ref = refs[:3]
     o_refs, (held, turned, packed, sems, out_sems) = refs[-5 - outs : -5], refs[-5:]
-    tiles = 4
+    tiles = 1
     tile = WIDTH // tiles
     copies = [
         pltpu.make_async_copy(
@@ -113,23 +116,25 @@
 def inner(weights, matrices, where, li, ri, shapes, after=()):
     hbm = pl.BlockSpec(memory_space=pltpu.HBM)
     count = len(matrices)
+    scalars = [where] if len(shapes) == 2 else []
     return pl.pallas_call(
         functools.partial(inner_kernel, matrices, len(shapes)),
-        in_specs=[pl.BlockSpec(memory_space=pltpu.SMEM), hbm, WHOLE, WHOLE]
+        in_specs=[pl.BlockSpec(memory_space=pltpu.SMEM)] * len(scalars)
+        + [hbm, WHOLE, WHOLE]
         + [ORDER] * len(after),
         out_specs=[hbm] * len(shapes),
         out_shape=shapes,
         scratch_shapes=[
-            pltpu.VMEM((4 * count, 128, WIDTH // 4), BF16),
+            pltpu.VMEM((1 * count, 128, WIDTH // 1), BF16),
             pltpu.VMEM((128 * PITCH, 128), F32),
             pltpu.VMEM((count, 128, BLOCKS, 128), BF16),
-            pltpu.SemaphoreType.DMA((4 * count,)),
+            pltpu.SemaphoreType.DMA((1 * count,)),
             pltpu.SemaphoreType.DMA((4 * count,)),
         ],
         compiler_params=pltpu.CompilerParams(vmem_limit_bytes=INNER_VMEM),
         cost_estimate=cost(4 * 128 * 128 * WIDTH, 2),
         name=f"inner{matrices[0]}",
-    )(where, weights, li, ri, *after)
+    )(*scalars, weights, li, ri, *after)
 
 
 def mix_blocks(refs, rows, ro):
@@ -318,7 +323,7 @@
 
 
 def last(x, lo, matrix, rotated, scales):
-    tile = 1792
+    tile = 7168
     return pl.pallas_call(
         last_kernel,
         grid=(WIDTH // tile,),
@@ -338,7 +343,7 @@
             pltpu.VMEM((128, 128), F32),
         ],
         input_output_aliases={2: 0, 3: 1},
-        compiler_params=pltpu.CompilerParams(vmem_limit_bytes=12 * MIB),
+        compiler_params=pltpu.CompilerParams(vmem_limit_bytes=24 * MIB),
         cost_estimate=cost(2 * 128 * 128 * WIDTH, 2),
         name=f"last{matrix}",
     )(lo, x, rotated, scales)
@@ -355,7 +360,7 @@
 
 
 def place(x, half, matrix, into=()):
-    tile = 1792
+    tile = 7168
     return pl.pallas_call(
         place_kernel,
         grid_spec=pltpu.PrefetchScalarGridSpec(
@@ -371,7 +376,7 @@
         ),
         out_shape=OUTPUTS,
         input_output_aliases={2: 0, 3: 1} if into else {},
-        compiler_params=pltpu.CompilerParams(vmem_limit_bytes=6 * MIB),
+        compiler_params=pltpu.CompilerParams(vmem_limit_bytes=12 * MIB),
         cost_estimate=cost(64 * WIDTH, 1),
         name=f"place{matrix}",
     )(half, x, *into)
@@ -412,10 +417,7 @@
     ro2 = jnp.where(xl == 0, ro, ro[::-1, :, :, ::-1]).reshape(2 * BLOCKS, 4 * BLOCKS)
 
     sent01_shape = jax.ShapeDtypeStruct((128, 2, BLOCKS, 128), BF16)
-    nowhere = jnp.zeros((2,), jnp.int32)
-    (sent01,) = inner(
-        weights, (0, 1), nowhere, left_inner, right_inner, [sent01_shape]
-    )
+    (sent01,) = inner(weights, (0, 1), None, left_inner, right_inner, [sent01_shape])
     came01 = lax.all_to_all(sent01, (XH, Y, Z, XL), 0, 0, tiled=True)
 
     keep2, send2 = inner(
@@ -423,11 +425,11 @@
     )
     came2 = swap(send2, XL)
     planes = right([keep2, came2, swap(keep2, CORE), swap(came2, CORE)], ro2)
-    planes = [planes[0]] + [
-        lax.ppermute(planes[d], (XH, XL), [(i, i ^ d) for i in range(4)])
-        for d in range(1, 4)
-    ]
-    sent2 = join(planes)
+    moved = {
+        d: lax.ppermute(planes[d], (XH, XL), [(i, i ^ d) for i in range(4)])
+        for d in (2, 1, 3)
+    }
+    sent2 = join([planes[0], moved[1], moved[2], moved[3]])
     came01 = gate(came01, [sent2])
     came2 = lax.all_to_all(sent2, (Y, Z), 0, 0, tiled=True)
 

time: 176 us -> 172 us (0.977)
  Pallas kernels: 38.9 us -> 32.6 us
  waiting for transfers between devices: 91.2 us -> 93.6 us
    pallas_call x4, Pallas kernels: 11.2 us -> 7.66 us  [place(): pl.pallas_call(place_kernel, grid_spec=pltpu.PrefetchScalarGridSpec(num_s...]
    pallas_call x2, Pallas kernels: 13.3 us -> 11.3 us  [inner(): pl.pallas_call(functools.partial(inner_kernel, matrices, len(shapes)), in...]
  transfers between devices with their start and end apart: 11 -> 11, of which waited for: 6 -> 6; matrix products, arithmetic and copies ran while one was open for 2% -> 2% of each run, Pallas kernels for 16% -> 14%
where the time goes in v3:
time: 172 us
  waiting for transfers between devices  93.6 us (54%)
  starting transfers between devices  38.6 us (22%)
  Pallas kernels  32.6 us (19%)
  local copies, waits for them, and re-layouts  4.95 us (3%)
    ppermute x6, waiting for transfers between devices, swap(): return lax.ppermute(x, axis, [(0, 1), (1, 0)])  45.5 us
    ppermute x3, waiting for transfers between devices, local(): lax.ppermute(planes[d], (XH, XL), [(i, i ^ d) for i in range(4)])  33 us
    all_to_all x1, starting transfers between devices, local(): came01 = lax.all_to_all(sent01, (XH, Y, Z, XL), 0, 0, tiled=True)  16.8 us
    all_to_all x1, waiting for transfers between devices, local(): came2 = lax.all_to_all(sent2, (Y, Z), 0, 0, tiled=True)  15.1 us
    pallas_call x2, Pallas kernels, inner(): pl.pallas_call(functools.partial(inner_kernel, matrices, len(shapes)), in...  11.3 us
    all_to_all x1, starting transfers between devices, local(): came2 = lax.all_to_all(sent2, (Y, Z), 0, 0, tiled=True)  10.1 us
    pallas_call x2, Pallas kernels, both(): pl.pallas_call(functools.partial(both_kernel, matrix), in_specs=[WHOLE, W...  7.82 us
    ppermute x6, starting transfers between devices, swap(): return lax.ppermute(x, axis, [(0, 1), (1, 0)])  7.73 us
  transfers between devices with their start and end apart: 11, of which 6 were waited for; matrix products, arithmetic and copies ran while one was open for 2% of the time, Pallas kernels for 14%

profile of v3, /device:TPU:1, one launch (start us, length us, event | category | flops | bytes accessed | tf_op | source)
XLA Modules:
  0.0 171.6 jit_solution(10284035217920899270)
XLA Ops:
  0.6 6.4 %inner0.1.refs_4_ = bf16[128,2,56,128]{3,2,1,0:T(8,128)(2,1)} custom-call(bf16[3,128,7168]{2,1,0:T(8,128)(2,1)} %refs_1_.3, bf16[128,128]{1,0:T(8,128)(2,1)} %refs_2_.3, bf16[128,128]{1,0:T(8,128)(2,1)} %refs_3_.1), custom_call_target="tpu_custom_call" | custom-call | flops 469762048 | bytes 3670016 | tf_op jit(solution)/shard_map/inner0/pallas_call | solution.py:120
  7.0 16.8 %all-to-all-start = ((bf16[128,2,56,128]{3,2,1,0:T(8,128)(2,1)}), bf16[128,2,56,128]{3,2,1,0:T(8,128)(2,1)}, u32[]{:S(2)}, u32[]{:S(2)}) async-start(bf16[128,2,56,128]{3,2,1,0:T(8,128)(2,1)} %inner0.1.refs_4_), calls=%async_computation | async-start | bytes 7340032 | tf_op jit(solution)/shard_map/all_to_all | solution.py:421
  23.9 0.6 pad_add_fusion.refs_0_
  24.5 4.9 %inner2.1 = (bf16[64,56,128]{2,1,0:T(8,128)(2,1)}, bf16[64,56,128]{2,1,0:T(8,128)(2,1)}) custom-call(s32[2]{0:T(128)} %pad_add_fusion.refs_0_, bf16[3,128,7168]{2,1,0:T(8,128)(2,1)} %refs_1_.3, bf16[128,128]{1,0:T(8,128)(2,1)} %refs_2_.3, bf16[128,128]{1,0:T(8,128)(2,1)} %refs_3_.1, bf16[128,2,56,128]{3,2,1,0:T(8,128)(2,1)} %inner0.1.refs_4_), custom_call_target="tpu_custom_call" | custom-call | flops 469762048 | bytes 3670016 | tf_op jit(solution)/shard_map/inner2/pallas_call | solution.py:120
  29.4 0.6 collective-permute-start
  30.0 1.5 collective-permute-start.1
  31.5 33.6 %collective-permute-done.refs_1_ = bf16[64,56,128]{2,1,0:T(8,128)(2,1)S(1)} collective-permute-done((bf16[64,56,128]{2,1,0:T(8,128)(2,1)}, bf16[64,56,128]{2,1,0:T(8,128)(2,1)S(1)}, u32[]{:S(2)}, u32[]{:S(2)}) %collective-permute-start) | collective-permute-done | bytes 917536 | tf_op jit(solution)/shard_map/ppermute | solution.py:398
  65.1 2.7 %collective-permute-start.2 = (bf16[64,56,128]{2,1,0:T(8,128)(2,1)S(1)}, bf16[64,56,128]{2,1,0:T(8,128)(2,1)S(1)}, u32[]{:S(2)}, u32[]{:S(2)}) collective-permute-start(bf16[64,56,128]{2,1,0:T(8,128)(2,1)S(1)} %collective-permute-done.refs_1_), channel_id=1, source_target_pairs={{0,1},{1,0},{2,3},{3,2},{4,5},{5,4},{6,7},{7,6},{8,9},{9,8},{10,11... | collective-permute-start | bytes 2752520 | tf_op jit(solution)/shard_map/ppermute | solution.py:398
  68.3 0.6 rev.17
  69.3 0.6 collective-permute-done.2.refs_3_
  69.9 1.2 copy-done.3
  71.0 1.9 %right.1 = (bf16[32,56,128]{2,1,0:T(8,128)(2,1)S(1)}, bf16[32,56,128]{2,1,0:T(8,128)(2,1)S(1)}, bf16[32,56,128]{2,1,0:T(8,128)(2,1)S(1)}, bf16[32,56,128]{2,1,0:T(8,128)(2,1)S(1)}) custom-call(bf16[112,224]{1,0:T(8,128)(2,1)S(1)} %reshape.31.ro_ref, bf16[64,56,128]{2,1,0:T(8,128)(2,1)S(1)} %copy-done.3, ...), custom_call_target="tpu_custom_call" | custom-call | flops 23060000768 | bytes 5505024 | tf_op jit(solution)/shard_map/right/pallas_call | solution.py:173
  73.0 1.0 collective-permute-start.3
  73.9 2.8 %collective-permute-start.4 = (bf16[32,56,128]{2,1,0:T(8,128)(2,1)S(1)}, bf16[32,56,128]{2,1,0:T(8,128)(2,1)S(1)}, u32[]{:S(2)}, u32[]{:S(2)}) collective-permute-start(bf16[32,56,128]{2,1,0:T(8,128)(2,1)S(1)} %get-tuple-element.26), channel_id=1, source_target_pairs={{0,128},{2,130},{128,0},{130,2},{1,129},{3,131},{129,1},{131,3},{4... | collective-permute-start | bytes 1376264 | tf_op jit(solution)/shard_map/ppermute | solution.py:429
  76.9 15.3 %collective-permute-done.3.refs_1_ = bf16[32,56,128]{2,1,0:T(8,128)(2,1)S(1)} collective-permute-done((bf16[32,56,128]{2,1,0:T(8,128)(2,1)S(1)}, bf16[32,56,128]{2,1,0:T(8,128)(2,1)S(1)}, u32[]{:S(2)}, u32[]{:S(2)}) %collective-permute-start.3) | collective-permute-done | bytes 458784 | tf_op jit(solution)/shard_map/ppermute | solution.py:429
  92.3 17.7 %collective-permute-done.4.refs_2_ = bf16[32,56,128]{2,1,0:T(8,128)(2,1)S(1)} collective-permute-done((bf16[32,56,128]{2,1,0:T(8,128)(2,1)S(1)}, bf16[32,56,128]{2,1,0:T(8,128)(2,1)S(1)}, u32[]{:S(2)}, u32[]{:S(2)}) %collective-permute-start.4) | collective-permute-done | bytes 458784 | tf_op jit(solution)/shard_map/ppermute | solution.py:429
  110.0 1.4 join.1.refs_1_
  111.4 1.4 collective-permute-start.6
  112.8 10.1 %all-to-all-start.1 = ((bf16[32,4,56,128]{3,2,1,0:T(8,128)(2,1)}), bf16[32,4,56,128]{3,2,1,0:T(8,128)(2,1)S(1)}, u32[]{:S(2)}, u32[]{:S(2)}) async-start(bf16[32,4,56,128]{3,2,1,0:T(8,128)(2,1)} %join.1.refs_1_), calls=%async_computation.1 | async-start | bytes 3670016 | tf_op jit(solution)/shard_map/all_to_all | solution.py:434
  123.1 3.9 %both0.1 = (bf16[64,7168]{1,0:T(8,128)(2,1)S(1)}, bf16[64,7168]{1,0:T(8,128)(2,1)}) custom-call(bf16[112,224]{1,0:T(8,128)(2,1)S(1)} %reshape.30.ro_ref, bf16[64,64]{1,0:T(8,128)(2,1)S(1)} %copy-done.2, bf16[128,2,56,128]{3,2,1,0:T(8,128)(2,1)} %gate.1.own_ref, bf16[128,2,56,128]{3,2,1,0:T(8,128)(2,1)} %collective-permute-done.6.other_ref), custom_call_target="tpu_custom_call" | custom-call | flops 256901120 | bytes 5505024 | tf_op jit(solution)/shard_map/both0/pallas_call | solution.py:266
  127.0 0.4 collective-permute-start.8
  127.4 3.9 %both1.1 = (bf16[64,7168]{1,0:T(8,128)(2,1)S(1)}, bf16[64,7168]{1,0:T(8,128)(2,1)}) custom-call(bf16[112,224]{1,0:T(8,128)(2,1)S(1)} %reshape.30.ro_ref, bf16[64,64]{1,0:T(8,128)(2,1)S(1)} %copy-done.2, bf16[128,2,56,128]{3,2,1,0:T(8,128)(2,1)} %gate.1.own_ref, bf16[128,2,56,128]{3,2,1,0:T(8,128)(2,1)} %collective-permute-done.6.other_ref), custom_call_target="tpu_custom_call" | custom-call | flops 256901120 | bytes 5505024 | tf_op jit(solution)/shard_map/both1/pallas_call | solution.py:266
  131.3 0.9 copy-done
  132.2 1.1 collective-permute-start.7
  134.0 1.3 place0.2
  135.3 1.2 copy-done.1
  136.5 1.3 place1.2
  137.8 11.2 %collective-permute-done.8.x_ref = bf16[64,7168]{1,0:T(8,128)(2,1)} collective-permute-done((bf16[64,7168]{1,0:T(8,128)(2,1)}, bf16[64,7168]{1,0:T(8,128)(2,1)}, u32[]{:S(2)}, u32[]{:S(2)}) %collective-permute-start.8) | collective-permute-done | bytes 917536 | tf_op jit(solution)/shard_map/ppermute | solution.py:398
  149.1 2.5 %place0.3 = (bf16[3,2,64,7168]{3,2,1,0:T(8,128)(2,1)}, f32[3,2,56,64]{3,2,1,0:T(8,128)}) custom-call(s32[1]{0:T(128)S(6)} %sub.4.half_ref, bf16[64,7168]{1,0:T(8,128)(2,1)} %collective-permute-done.8.x_ref, bf16[3,2,64,7168]{3,2,1,0:T(8,128)(2,1)} %get-tuple-element.34.refs_0_, ...), custom_call_target="tpu_custom_call", output_to_operand_aliasing={{0}: (2, {}), {1}: (3, {})} | custom-call | flops 458752 | bytes 1835008 | tf_op jit(solution)/shard_map/place0/pallas_call | solution.py:364
  151.6 15.1 %all-to-all-done.1 = bf16[32,4,56,128]{3,2,1,0:T(8,128)(2,1)S(1)} async-done(((bf16[32,4,56,128]{3,2,1,0:T(8,128)(2,1)}), bf16[32,4,56,128]{3,2,1,0:T(8,128)(2,1)S(1)}, u32[]{:S(2)}, u32[]{:S(2)}) %all-to-all-start.1) | async-done | bytes 1835040 | tf_op jit(solution)/shard_map/all_to_all | solution.py:434
  166.7 2.5 %last2.1 = (bf16[3,2,64,7168]{3,2,1,0:T(8,128)(2,1)}, f32[3,2,56,64]{3,2,1,0:T(8,128)}) custom-call(bf16[128,128]{1,0:T(8,128)(2,1)S(1)} %copy.23.lo_ref, bf16[128,56,128]{2,1,0:T(8,128)(2,1)S(1)} %bitcast.13, bf16[3,2,64,7168]{3,2,1,0:T(8,128)(2,1)} %get-tuple-element.36.refs_0_, ...), custom_call_target="tpu_custom_call", output_to_operand_aliasing={{0}: (2, {}), {1}: (3, {})} | custom-call | flops 234881024 | bytes 3670016 | tf_op jit(solution)/shard_map/last2/pallas_call | solution.py:327
  169.1 2.5 %place1.3 = (bf16[3,2,64,7168]{3,2,1,0:T(8,128)(2,1)}, f32[3,2,56,64]{3,2,1,0:T(8,128)}) custom-call(s32[1]{0:T(128)S(6)} %sub.4.half_ref, bf16[64,7168]{1,0:T(8,128)(2,1)} %collective-permute-done.7.x_ref, bf16[3,2,64,7168]{3,2,1,0:T(8,128)(2,1)} %get-tuple-element.38.refs_0_, ...), custom_call_target="tpu_custom_call", output_to_operand_aliasing={{0}: (2, {}), {1}: (3, {})} | custom-call | flops 458752 | bytes 1835008 | tf_op jit(solution)/shard_map/place1/pallas_call | solution.py:364
  (30 shorter events, 1.7 us)
Async XLA Ops:
  7.0 104.3 %all-to-all-start = ((bf16[128,2,56,128]{3,2,1,0:T(8,128)(2,1)}), bf16[128,2,56,128]{3,2,1,0:T(8,128)(2,1)}, u32[]{:S(2)}, u32[]{:S(2)}) async-start(bf16[128,2,56,128]{3,2,1,0:T(8,128)(2,1)} %inner0.1.refs_4_), calls=%async_computation | async-start | bytes 7340032 | tf_op jit(solution)/shard_map/all_to_all | solution.py:421
  23.9 43.9 %copy-start.4 = (bf16[224,224]{1,0:T(8,128)(2,1)S(1)}, bf16[224,224]{1,0:T(8,128)(2,1)}, u32[]{:S(2)}) copy-start(bf16[224,224]{1,0:T(8,128)(2,1)} %param.8) | copy-start | bytes 301060
  29.4 35.7 %collective-permute-start = (bf16[64,56,128]{2,1,0:T(8,128)(2,1)}, bf16[64,56,128]{2,1,0:T(8,128)(2,1)S(1)}, u32[]{:S(2)}, u32[]{:S(2)}) collective-permute-start(bf16[64,56,128]{2,1,0:T(8,128)(2,1)} %get-tuple-element.23), channel_id=1, source_target_pairs={{0,2},{2,0},{1,3},{3,1},{4,6},{6,4},{5,7},{7,5},{8,10},{10,8},{9,1... | collective-permute-start | bytes 2752520 | tf_op jit(solution)/shard_map/ppermute | solution.py:398
  30.0 39.3 %collective-permute-start.1 = (bf16[64,56,128]{2,1,0:T(8,128)(2,1)}, bf16[64,56,128]{2,1,0:T(8,128)(2,1)S(1)}, u32[]{:S(2)}, u32[]{:S(2)}) collective-permute-start(bf16[64,56,128]{2,1,0:T(8,128)(2,1)} %get-tuple-element.22.refs_0_), channel_id=1, source_target_pairs={{0,1},{1,0},{2,3},{3,2},{4,5},{5,4},{6,7},{7,6},{8,9},{9,8},{10,11... | collective-permute-start | bytes 2752520 | tf_op jit(solution)/shard_map/ppermute | solution.py:398
  65.1 4.8 %collective-permute-start.2 = (bf16[64,56,128]{2,1,0:T(8,128)(2,1)S(1)}, bf16[64,56,128]{2,1,0:T(8,128)(2,1)S(1)}, u32[]{:S(2)}, u32[]{:S(2)}) collective-permute-start(bf16[64,56,128]{2,1,0:T(8,128)(2,1)S(1)} %collective-permute-done.refs_1_), channel_id=1, source_target_pairs={{0,1},{1,0},{2,3},{3,2},{4,5},{5,4},{6,7},{7,6},{8,9},{9,8},{10,11... | collective-permute-start | bytes 2752520 | tf_op jit(solution)/shard_map/ppermute | solution.py:398
  69.9 1.2 copy-start.3
  73.0 19.3 %collective-permute-start.3 = (bf16[32,56,128]{2,1,0:T(8,128)(2,1)S(1)}, bf16[32,56,128]{2,1,0:T(8,128)(2,1)S(1)}, u32[]{:S(2)}, u32[]{:S(2)}) collective-permute-start(bf16[32,56,128]{2,1,0:T(8,128)(2,1)S(1)} %get-tuple-element.25), channel_id=1, source_target_pairs={{0,2},{2,0},{128,130},{130,128},{1,3},{3,1},{129,131},{131,129},{4... | collective-permute-start | bytes 1376264 | tf_op jit(solution)/shard_map/ppermute | solution.py:429
  73.9 36.0 %collective-permute-start.4 = (bf16[32,56,128]{2,1,0:T(8,128)(2,1)S(1)}, bf16[32,56,128]{2,1,0:T(8,128)(2,1)S(1)}, u32[]{:S(2)}, u32[]{:S(2)}) collective-permute-start(bf16[32,56,128]{2,1,0:T(8,128)(2,1)S(1)} %get-tuple-element.26), channel_id=1, source_target_pairs={{0,128},{2,130},{128,0},{130,2},{1,129},{3,131},{129,1},{131,3},{4... | collective-permute-start | bytes 1376264 | tf_op jit(solution)/shard_map/ppermute | solution.py:429
  76.7 33.2 %collective-permute-start.5 = (bf16[32,56,128]{2,1,0:T(8,128)(2,1)S(1)}, bf16[32,56,128]{2,1,0:T(8,128)(2,1)S(1)}, u32[]{:S(2)}, u32[]{:S(2)}) collective-permute-start(bf16[32,56,128]{2,1,0:T(8,128)(2,1)S(1)} %get-tuple-element.27), channel_id=1, source_target_pairs={{0,130},{2,128},{128,2},{130,0},{1,131},{3,129},{129,3},{131,1},{4... | collective-permute-start | bytes 1376264 | tf_op jit(solution)/shard_map/ppermute | solution.py:429
  111.4 11.7 %copy-start.2 = (bf16[64,64]{1,0:T(8,128)(2,1)S(1)}, bf16[64,64]{1,0:T(8,128)(2,1)}, u32[]{:S(2)}) copy-start(bf16[64,64]{1,0:T(8,128)(2,1)} %lo_ref.3) | copy-start | bytes 24580
  111.4 11.7 %collective-permute-start.6 = (bf16[128,2,56,128]{3,2,1,0:T(8,128)(2,1)}, bf16[128,2,56,128]{3,2,1,0:T(8,128)(2,1)}, u32[]{:S(2)}, u32[]{:S(2)}) collective-permute-start(bf16[128,2,56,128]{3,2,1,0:T(8,128)(2,1)} %gate.1.own_ref), channel_id=1, source_target_pairs={{0,1},{1,0},{2,3},{3,2},{4,5},{5,4},{6,7},{7,6},{8,9},{9,8},{10,11... | collective-permute-start | bytes 11010056 | tf_op jit(solution)/shard_map/ppermute | solution.py:398
  112.8 53.9 %all-to-all-start.1 = ((bf16[32,4,56,128]{3,2,1,0:T(8,128)(2,1)}), bf16[32,4,56,128]{3,2,1,0:T(8,128)(2,1)S(1)}, u32[]{:S(2)}, u32[]{:S(2)}) async-start(bf16[32,4,56,128]{3,2,1,0:T(8,128)(2,1)} %join.1.refs_1_), calls=%async_computation.1 | async-start | bytes 3670016 | tf_op jit(solution)/shard_map/all_to_all | solution.py:434
  127.0 22.1 %collective-permute-start.8 = (bf16[64,7168]{1,0:T(8,128)(2,1)}, bf16[64,7168]{1,0:T(8,128)(2,1)}, u32[]{:S(2)}, u32[]{:S(2)}) collective-permute-start(bf16[64,7168]{1,0:T(8,128)(2,1)} %get-tuple-element.29), channel_id=1, source_target_pairs={{0,2},{2,0},{1,3},{3,1},{4,6},{6,4},{5,7},{7,5},{8,10},{10,8},{9,1... | collective-permute-start | bytes 2752520 | tf_op jit(solution)/shard_map/ppermute | solution.py:398
  131.3 0.9 copy-start
  132.2 36.9 %collective-permute-start.7 = (bf16[64,7168]{1,0:T(8,128)(2,1)}, bf16[64,7168]{1,0:T(8,128)(2,1)}, u32[]{:S(2)}, u32[]{:S(2)}) collective-permute-start(bf16[64,7168]{1,0:T(8,128)(2,1)} %get-tuple-element.28), channel_id=1, source_target_pairs={{0,2},{2,0},{1,3},{3,1},{4,6},{6,4},{5,7},{7,5},{8,10},{10,8},{9,1... | collective-permute-start | bytes 2752520 | tf_op jit(solution)/shard_map/ppermute | solution.py:398
  135.3 1.2 copy-start.1

commit v4 on v3

--- a/solution.py
+++ b/solution.py
@@ -218,7 +218,7 @@
 
 
 def both_kernel(matrix, ro_ref, lo_ref, own_ref, other_ref, *refs):
-    o_refs, (held, turned, sems) = refs[-5:-3], refs[-3:]
+    o_ref, held, turned, sems = refs[-4:]
     arriving = [
         [
             pltpu.make_async_copy(
@@ -243,40 +243,37 @@
         where = [[(at, 2 * r + half) for at in (0, 1) for half in (0, 1)] for r in rows]
         mixed = mix_blocks([held] * 4, where, ro)
         for at, r in enumerate(rows):
-            turned[pl.ds(r, 2 * BLOCKS, stride=stride), :] = mixed[
+            turned[pl.ds(r, BLOCKS, stride=stride), :] = mixed[
                 :, at * 128 : at * 128 + 128
             ]
     lo = lo_ref[...]
-    for half, ref in enumerate(o_refs):
-        for first in range(0, BLOCKS, 14):
-            x = jnp.concatenate(
-                [
-                    turned[
-                        (half * BLOCKS + p) * stride : (half * BLOCKS + p) * stride + 64, :
-                    ].astype(BF16)
-                    for p in range(first, first + 14)
-                ],
-                axis=1,
-            )
-            ref[:, first * 128 : (first + 14) * 128] = matmul(lo, x).astype(BF16)
-
-
-def both(own, other, matrix, ro, lo):
+    for first in range(0, BLOCKS, 14):
+        x = jnp.concatenate(
+            [
+                turned[p * stride : p * stride + 64, :].astype(BF16)
+                for p in range(first, first + 14)
+            ],
+            axis=1,
+        )
+        o_ref[:, first * 128 : (first + 14) * 128] = matmul(lo, x).astype(BF16)
+
+
+def both(own, other, matrix, ro, lo, after=()):
     hbm = pl.BlockSpec(memory_space=pltpu.HBM)
     return pl.pallas_call(
         functools.partial(both_kernel, matrix),
-        in_specs=[WHOLE, WHOLE, hbm, hbm],
-        out_specs=[WHOLE] * 2,
-        out_shape=[jax.ShapeDtypeStruct((64, WIDTH), BF16)] * 2,
+        in_specs=[WHOLE, WHOLE, hbm, hbm] + [ORDER] * len(after),
+        out_specs=WHOLE,
+        out_shape=jax.ShapeDtypeStruct((64, WIDTH), BF16),
         scratch_shapes=[
             pltpu.VMEM((2, 128, BLOCKS, 128), BF16),
-            pltpu.VMEM((2 * BLOCKS * 73, 128), F32),
+            pltpu.VMEM((BLOCKS * 73, 128), F32),
             pltpu.SemaphoreType.DMA((2, 4)),
         ],
         compiler_params=pltpu.CompilerParams(vmem_limit_bytes=18 * MIB),
         cost_estimate=cost(10 * 64 * BLOCKS * WIDTH, 3),
         name=f"both{matrix}",
-    )(ro, lo, own, other)
+    )(ro, lo, own, other, *after)
 
 
 def block_scales(values, first, held):
@@ -434,13 +431,16 @@
     came2 = lax.all_to_all(sent2, (Y, Z), 0, 0, tiled=True)
 
     other01 = swap(came01, CORE)
-    own0, send0 = both(came01, other01, 0, ro01, left_outer)
-    own1, send1 = both(came01, other01, 1, ro01, left_outer)
+    ro_own, ro_partner = ro01[:BLOCKS], ro01[BLOCKS:]
+    send0 = both(came01, other01, 0, ro_partner, left_outer)
+    send1 = both(came01, other01, 1, ro_partner, left_outer, [send0])
+    own0 = both(came01, other01, 0, ro_own, left_outer, [send1])
+    own1 = both(came01, other01, 1, ro_own, left_outer, [own0])
     outputs = place(own0, own_half, 0)
     outputs = place(own1, own_half, 1, outputs)
     outputs = place(swap(send0, XL), 1 - own_half, 0, outputs)
-    outputs = last(came2.reshape(128, BLOCKS, 128), lo2, 2, *outputs)
-    rotated, scales = place(swap(send1, XL), 1 - own_half, 1, outputs)
+    outputs = place(swap(send1, XL), 1 - own_half, 1, outputs)
+    rotated, scales = last(came2.reshape(128, BLOCKS, 128), lo2, 2, *outputs)
     return rotated, scales.transpose(0, 1, 3, 2)
 
 

time: 172 us -> 174 us (1.012)
  Pallas kernels: 32.6 us -> 37.5 us
  local copies, waits for them, and re-layouts: 4.95 us -> 3 us
    all_to_all x1, waiting for transfers between devices: 15.1 us -> 0.01 us  [local(): came2 = lax.all_to_all(sent2, (Y, Z), 0, 0, tiled=True)]
    ppermute x6, waiting for transfers between devices: 45.5 us -> 59.3 us  [swap(): return lax.ppermute(x, axis, [(0, 1), (1, 0)])]
    pallas_call x2 -> x4, Pallas kernels: 7.82 us -> 12.8 us  [both(): pl.pallas_call(functools.partial(both_kernel, matrix), in_specs=[WHOLE, W...]
    unnamed x12 -> x8, local copies, waits for them, and re-layouts: 3.46 us -> 1.36 us
  transfers between devices with their start and end apart: 11 -> 11, of which waited for: 6 -> 6; matrix products, arithmetic and copies ran while one was open for 2% -> 2% of each run, Pallas kernels for 14% -> 17%
where the time goes in v4:
time: 174 us; the launch traced here: 173 us
  waiting for transfers between devices  92.3 us (53%)
  starting transfers between devices  38.7 us (22%)
  Pallas kernels  37.5 us (22%)
  local copies, waits for them, and re-layouts  3 us (2%)
    ppermute x6, waiting for transfers between devices, swap(): return lax.ppermute(x, axis, [(0, 1), (1, 0)])  59.3 us
    ppermute x3, waiting for transfers between devices, local(): lax.ppermute(planes[d], (XH, XL), [(i, i ^ d) for i in range(4)])  33 us
    all_to_all x1, starting transfers between devices, local(): came01 = lax.all_to_all(sent01, (XH, Y, Z, XL), 0, 0, tiled=True)  16.8 us
    pallas_call x4, Pallas kernels, both(): pl.pallas_call(functools.partial(both_kernel, matrix), in_specs=[WHOLE, W...  12.8 us
    pallas_call x2, Pallas kernels, inner(): pl.pallas_call(functools.partial(inner_kernel, matrices, len(shapes)), in...  11.3 us
    all_to_all x1, starting transfers between devices, local(): came2 = lax.all_to_all(sent2, (Y, Z), 0, 0, tiled=True)  10.1 us
    ppermute x6, starting transfers between devices, swap(): return lax.ppermute(x, axis, [(0, 1), (1, 0)])  7.8 us
    pallas_call x4, Pallas kernels, place(): pl.pallas_call(place_kernel, grid_spec=pltpu.PrefetchScalarGridSpec(num_s...  7.66 us
  transfers between devices with their start and end apart: 11, of which 6 were waited for; matrix products, arithmetic and copies ran while one was open for 2% of the time, Pallas kernels for 17%

profile of v4, /device:TPU:1, one launch (start us, length us, event | category | flops | bytes accessed | tf_op | source)
XLA Modules:
  0.0 173.5 jit_solution(2470275686157183283)
XLA Ops:
  0.6 6.4 %inner0.1.refs_4_ = bf16[128,2,56,128]{3,2,1,0:T(8,128)(2,1)} custom-call(bf16[3,128,7168]{2,1,0:T(8,128)(2,1)} %refs_1_.3, bf16[128,128]{1,0:T(8,128)(2,1)} %refs_2_.3, bf16[128,128]{1,0:T(8,128)(2,1)} %refs_3_.1), custom_call_target="tpu_custom_call" | custom-call | flops 469762048 | bytes 3670016 | tf_op jit(solution)/shard_map/inner0/pallas_call | solution.py:120
  7.0 16.8 %all-to-all-start.1 = ((bf16[128,2,56,128]{3,2,1,0:T(8,128)(2,1)}), bf16[128,2,56,128]{3,2,1,0:T(8,128)(2,1)}, u32[]{:S(2)}, u32[]{:S(2)}) async-start(bf16[128,2,56,128]{3,2,1,0:T(8,128)(2,1)} %inner0.1.refs_4_), calls=%async_computation.1 | async-start | bytes 7340032 | tf_op jit(solution)/shard_map/all_to_all | solution.py:418
  23.9 0.6 pad_add_fusion.refs_0_
  24.5 4.9 %inner2.1 = (bf16[64,56,128]{2,1,0:T(8,128)(2,1)}, bf16[64,56,128]{2,1,0:T(8,128)(2,1)}) custom-call(s32[2]{0:T(128)} %pad_add_fusion.refs_0_, bf16[3,128,7168]{2,1,0:T(8,128)(2,1)} %refs_1_.3, bf16[128,128]{1,0:T(8,128)(2,1)} %refs_2_.3, bf16[128,128]{1,0:T(8,128)(2,1)} %refs_3_.1, bf16[128,2,56,128]{3,2,1,0:T(8,128)(2,1)} %inner0.1.refs_4_), custom_call_target="tpu_custom_call" | custom-call | flops 469762048 | bytes 3670016 | tf_op jit(solution)/shard_map/inner2/pallas_call | solution.py:120
  29.4 0.6 collective-permute-start
  30.0 1.5 collective-permute-start.1
  31.5 33.6 %collective-permute-done.refs_1_ = bf16[64,56,128]{2,1,0:T(8,128)(2,1)S(1)} collective-permute-done((bf16[64,56,128]{2,1,0:T(8,128)(2,1)}, bf16[64,56,128]{2,1,0:T(8,128)(2,1)S(1)}, u32[]{:S(2)}, u32[]{:S(2)}) %collective-permute-start) | collective-permute-done | bytes 917536 | tf_op jit(solution)/shard_map/ppermute | solution.py:395
  65.1 2.6 %collective-permute-start.2 = (bf16[64,56,128]{2,1,0:T(8,128)(2,1)S(1)}, bf16[64,56,128]{2,1,0:T(8,128)(2,1)S(1)}, u32[]{:S(2)}, u32[]{:S(2)}) collective-permute-start(bf16[64,56,128]{2,1,0:T(8,128)(2,1)S(1)} %collective-permute-done.refs_1_), channel_id=1, source_target_pairs={{0,1},{1,0},{2,3},{3,2},{4,5},{5,4},{6,7},{7,6},{8,9},{9,8},{10,11... | collective-permute-start | bytes 2752520 | tf_op jit(solution)/shard_map/ppermute | solution.py:395
  68.3 0.6 rev.18
  69.3 0.6 collective-permute-done.2.refs_3_
  69.9 1.2 copy-done.1
  71.0 1.9 %right.1 = (bf16[32,56,128]{2,1,0:T(8,128)(2,1)S(1)}, bf16[32,56,128]{2,1,0:T(8,128)(2,1)S(1)}, bf16[32,56,128]{2,1,0:T(8,128)(2,1)S(1)}, bf16[32,56,128]{2,1,0:T(8,128)(2,1)S(1)}) custom-call(bf16[112,224]{1,0:T(8,128)(2,1)S(1)} %reshape.31.ro_ref, bf16[64,56,128]{2,1,0:T(8,128)(2,1)S(1)} %copy-done.1, ...), custom_call_target="tpu_custom_call" | custom-call | flops 23060000768 | bytes 5505024 | tf_op jit(solution)/shard_map/right/pallas_call | solution.py:173
  73.0 1.0 collective-permute-start.3
  73.9 2.8 %collective-permute-start.4 = (bf16[32,56,128]{2,1,0:T(8,128)(2,1)S(1)}, bf16[32,56,128]{2,1,0:T(8,128)(2,1)S(1)}, u32[]{:S(2)}, u32[]{:S(2)}) collective-permute-start(bf16[32,56,128]{2,1,0:T(8,128)(2,1)S(1)} %get-tuple-element.22), channel_id=1, source_target_pairs={{0,128},{2,130},{128,0},{130,2},{1,129},{3,131},{129,1},{131,3},{4... | collective-permute-start | bytes 1376264 | tf_op jit(solution)/shard_map/ppermute | solution.py:426
  76.9 15.3 %collective-permute-done.3.refs_1_ = bf16[32,56,128]{2,1,0:T(8,128)(2,1)S(1)} collective-permute-done((bf16[32,56,128]{2,1,0:T(8,128)(2,1)S(1)}, bf16[32,56,128]{2,1,0:T(8,128)(2,1)S(1)}, u32[]{:S(2)}, u32[]{:S(2)}) %collective-permute-start.3) | collective-permute-done | bytes 458784 | tf_op jit(solution)/shard_map/ppermute | solution.py:426
  92.3 17.7 %collective-permute-done.4.refs_2_ = bf16[32,56,128]{2,1,0:T(8,128)(2,1)S(1)} collective-permute-done((bf16[32,56,128]{2,1,0:T(8,128)(2,1)S(1)}, bf16[32,56,128]{2,1,0:T(8,128)(2,1)S(1)}, u32[]{:S(2)}, u32[]{:S(2)}) %collective-permute-start.4) | collective-permute-done | bytes 458784 | tf_op jit(solution)/shard_map/ppermute | solution.py:426
  109.9 1.4 join.1.refs_1_
  111.4 1.4 collective-permute-start.6
  112.8 10.1 %all-to-all-start = ((bf16[32,4,56,128]{3,2,1,0:T(8,128)(2,1)}), bf16[32,4,56,128]{3,2,1,0:T(8,128)(2,1)S(1)}, u32[]{:S(2)}, u32[]{:S(2)}) async-start(bf16[32,4,56,128]{3,2,1,0:T(8,128)(2,1)} %join.1.refs_1_), calls=%async_computation | async-start | bytes 3670016 | tf_op jit(solution)/shard_map/all_to_all | solution.py:431
  123.1 3.7 %both0.2.refs_0_ = bf16[64,7168]{1,0:T(8,128)(2,1)} custom-call(bf16[56,224]{1,0:T(8,128)(2,1)S(1)} %slice.21.ro_ref, bf16[64,64]{1,0:T(8,128)(2,1)S(1)} %copy-done, bf16[128,2,56,128]{3,2,1,0:T(8,128)(2,1)} %gate.1.own_ref, bf16[128,2,56,128]{3,2,1,0:T(8,128)(2,1)} %collective-permute-done.6.other_ref), custom_call_target="tpu_custom_call" | custom-call | flops 256901120 | bytes 5505024 | tf_op jit(solution)/shard_map/both0/pallas_call | solution.py:263
  126.8 0.4 collective-permute-start.8
  127.2 3.7 %both1.2.refs_0_ = bf16[64,7168]{1,0:T(8,128)(2,1)} custom-call(bf16[56,224]{1,0:T(8,128)(2,1)S(1)} %slice.21.ro_ref, bf16[64,64]{1,0:T(8,128)(2,1)S(1)} %copy-done, bf16[128,2,56,128]{3,2,1,0:T(8,128)(2,1)} %gate.1.own_ref, bf16[128,2,56,128]{3,2,1,0:T(8,128)(2,1)} %collective-permute-done.6.other_ref, bf16[64,7168]{1,0:T(8,128)(2,1)} %both0.2.refs_0_), custom_call_target="tpu_custom_call" | custom-call | flops 256901120 | bytes 5505024 | tf_op jit(solution)/shard_map/both1/pallas_call | solution.py:263
  130.9 1.2 collective-permute-start.7
  132.7 2.7 %both0.3.refs_0_.x_ref = bf16[64,7168]{1,0:T(8,128)(2,1)S(1)} custom-call(bf16[56,224]{1,0:T(8,128)(2,1)S(1)} %slice.23.ro_ref, bf16[64,64]{1,0:T(8,128)(2,1)S(1)} %copy-done, bf16[128,2,56,128]{3,2,1,0:T(8,128)(2,1)} %gate.1.own_ref, bf16[128,2,56,128]{3,2,1,0:T(8,128)(2,1)} %collective-permute-done.6.other_ref, bf16[64,7168]{1,0:T(8,128)(2,1)} %both1.2.refs_0_), custom_call_target="tpu_custom_call" | custom-call | flops 256901120 | bytes 5505024 | tf_op jit(solution)/shard_map/both0/pallas_call | solution.py:263
  135.6 1.3 place0.2
  136.9 2.7 %both1.3.x_ref = bf16[64,7168]{1,0:T(8,128)(2,1)S(1)} custom-call(bf16[56,224]{1,0:T(8,128)(2,1)S(1)} %slice.23.ro_ref, bf16[64,64]{1,0:T(8,128)(2,1)S(1)} %copy-done, bf16[128,2,56,128]{3,2,1,0:T(8,128)(2,1)} %gate.1.own_ref, bf16[128,2,56,128]{3,2,1,0:T(8,128)(2,1)} %collective-permute-done.6.other_ref, bf16[64,7168]{1,0:T(8,128)(2,1)S(1)} %both0.3.refs_0_.x_ref), custom_call_target="tpu_custom_call" | custom-call | flops 256901120 | bytes 5505024 | tf_op jit(solution)/shard_map/both1/pallas_call | solution.py:263
  139.6 1.3 place1.2
  141.0 7.9 %collective-permute-done.8.x_ref = bf16[64,7168]{1,0:T(8,128)(2,1)} collective-permute-done((bf16[64,7168]{1,0:T(8,128)(2,1)}, bf16[64,7168]{1,0:T(8,128)(2,1)}, u32[]{:S(2)}, u32[]{:S(2)}) %collective-permute-start.8) | collective-permute-done | bytes 917536 | tf_op jit(solution)/shard_map/ppermute | solution.py:395
  148.8 2.5 %place0.3 = (bf16[3,2,64,7168]{3,2,1,0:T(8,128)(2,1)}, f32[3,2,56,64]{3,2,1,0:T(8,128)}) custom-call(s32[1]{0:T(128)S(6)} %sub.4.half_ref, bf16[64,7168]{1,0:T(8,128)(2,1)} %collective-permute-done.8.x_ref, bf16[3,2,64,7168]{3,2,1,0:T(8,128)(2,1)} %get-tuple-element.26.refs_0_, ...), custom_call_target="tpu_custom_call", output_to_operand_aliasing={{0}: (2, {}), {1}: (3, {})} | custom-call | flops 458752 | bytes 1835008 | tf_op jit(solution)/shard_map/place0/pallas_call | solution.py:361
  151.3 17.2 %collective-permute-done.7.x_ref = bf16[64,7168]{1,0:T(8,128)(2,1)} collective-permute-done((bf16[64,7168]{1,0:T(8,128)(2,1)}, bf16[64,7168]{1,0:T(8,128)(2,1)}, u32[]{:S(2)}, u32[]{:S(2)}) %collective-permute-start.7) | collective-permute-done | bytes 917536 | tf_op jit(solution)/shard_map/ppermute | solution.py:395
  168.5 2.5 %place1.3 = (bf16[3,2,64,7168]{3,2,1,0:T(8,128)(2,1)}, f32[3,2,56,64]{3,2,1,0:T(8,128)}) custom-call(s32[1]{0:T(128)S(6)} %sub.4.half_ref, bf16[64,7168]{1,0:T(8,128)(2,1)} %collective-permute-done.7.x_ref, bf16[3,2,64,7168]{3,2,1,0:T(8,128)(2,1)} %get-tuple-element.28.refs_0_, ...), custom_call_target="tpu_custom_call", output_to_operand_aliasing={{0}: (2, {}), {1}: (3, {})} | custom-call | flops 458752 | bytes 1835008 | tf_op jit(solution)/shard_map/place1/pallas_call | solution.py:361
  171.0 2.5 %last2.1 = (bf16[3,2,64,7168]{3,2,1,0:T(8,128)(2,1)}, f32[3,2,56,64]{3,2,1,0:T(8,128)}) custom-call(bf16[128,128]{1,0:T(8,128)(2,1)S(1)} %copy.23.lo_ref, bf16[128,56,128]{2,1,0:T(8,128)(2,1)S(1)} %bitcast.13, bf16[3,2,64,7168]{3,2,1,0:T(8,128)(2,1)} %get-tuple-element.30.refs_0_, ...), custom_call_target="tpu_custom_call", output_to_operand_aliasing={{0}: (2, {}), {1}: (3, {})} | custom-call | flops 234881024 | bytes 3670016 | tf_op jit(solution)/shard_map/last2/pallas_call | solution.py:324
  (30 shorter events, 1.9 us)
Async XLA Ops:
  7.0 104.3 %all-to-all-start.1 = ((bf16[128,2,56,128]{3,2,1,0:T(8,128)(2,1)}), bf16[128,2,56,128]{3,2,1,0:T(8,128)(2,1)}, u32[]{:S(2)}, u32[]{:S(2)}) async-start(bf16[128,2,56,128]{3,2,1,0:T(8,128)(2,1)} %inner0.1.refs_4_), calls=%async_computation.1 | async-start | bytes 7340032 | tf_op jit(solution)/shard_map/all_to_all | solution.py:418
  23.9 43.9 %copy-start.2 = (bf16[224,224]{1,0:T(8,128)(2,1)S(1)}, bf16[224,224]{1,0:T(8,128)(2,1)}, u32[]{:S(2)}) copy-start(bf16[224,224]{1,0:T(8,128)(2,1)} %param.8) | copy-start | bytes 301060
  29.4 35.7 %collective-permute-start = (bf16[64,56,128]{2,1,0:T(8,128)(2,1)}, bf16[64,56,128]{2,1,0:T(8,128)(2,1)S(1)}, u32[]{:S(2)}, u32[]{:S(2)}) collective-permute-start(bf16[64,56,128]{2,1,0:T(8,128)(2,1)} %get-tuple-element.19), channel_id=1, source_target_pairs={{0,2},{2,0},{1,3},{3,1},{4,6},{6,4},{5,7},{7,5},{8,10},{10,8},{9,1... | collective-permute-start | bytes 2752520 | tf_op jit(solution)/shard_map/ppermute | solution.py:395
  30.0 39.3 %collective-permute-start.1 = (bf16[64,56,128]{2,1,0:T(8,128)(2,1)}, bf16[64,56,128]{2,1,0:T(8,128)(2,1)S(1)}, u32[]{:S(2)}, u32[]{:S(2)}) collective-permute-start(bf16[64,56,128]{2,1,0:T(8,128)(2,1)} %get-tuple-element.18.refs_0_), channel_id=1, source_target_pairs={{0,1},{1,0},{2,3},{3,2},{4,5},{5,4},{6,7},{7,6},{8,9},{9,8},{10,11... | collective-permute-start | bytes 2752520 | tf_op jit(solution)/shard_map/ppermute | solution.py:395
  65.1 4.7 %collective-permute-start.2 = (bf16[64,56,128]{2,1,0:T(8,128)(2,1)S(1)}, bf16[64,56,128]{2,1,0:T(8,128)(2,1)S(1)}, u32[]{:S(2)}, u32[]{:S(2)}) collective-permute-start(bf16[64,56,128]{2,1,0:T(8,128)(2,1)S(1)} %collective-permute-done.refs_1_), channel_id=1, source_target_pairs={{0,1},{1,0},{2,3},{3,2},{4,5},{5,4},{6,7},{7,6},{8,9},{9,8},{10,11... | collective-permute-start | bytes 2752520 | tf_op jit(solution)/shard_map/ppermute | solution.py:395
  69.9 1.2 copy-start.1
  73.0 19.3 %collective-permute-start.3 = (bf16[32,56,128]{2,1,0:T(8,128)(2,1)S(1)}, bf16[32,56,128]{2,1,0:T(8,128)(2,1)S(1)}, u32[]{:S(2)}, u32[]{:S(2)}) collective-permute-start(bf16[32,56,128]{2,1,0:T(8,128)(2,1)S(1)} %get-tuple-element.21), channel_id=1, source_target_pairs={{0,2},{2,0},{128,130},{130,128},{1,3},{3,1},{129,131},{131,129},{4... | collective-permute-start | bytes 1376264 | tf_op jit(solution)/shard_map/ppermute | solution.py:426
  73.9 36.0 %collective-permute-start.4 = (bf16[32,56,128]{2,1,0:T(8,128)(2,1)S(1)}, bf16[32,56,128]{2,1,0:T(8,128)(2,1)S(1)}, u32[]{:S(2)}, u32[]{:S(2)}) collective-permute-start(bf16[32,56,128]{2,1,0:T(8,128)(2,1)S(1)} %get-tuple-element.22), channel_id=1, source_target_pairs={{0,128},{2,130},{128,0},{130,2},{1,129},{3,131},{129,1},{131,3},{4... | collective-permute-start | bytes 1376264 | tf_op jit(solution)/shard_map/ppermute | solution.py:426
  76.7 33.3 %collective-permute-start.5 = (bf16[32,56,128]{2,1,0:T(8,128)(2,1)S(1)}, bf16[32,56,128]{2,1,0:T(8,128)(2,1)S(1)}, u32[]{:S(2)}, u32[]{:S(2)}) collective-permute-start(bf16[32,56,128]{2,1,0:T(8,128)(2,1)S(1)} %get-tuple-element.23), channel_id=1, source_target_pairs={{0,130},{2,128},{128,2},{130,0},{1,131},{3,129},{129,3},{131,1},{4... | collective-permute-start | bytes 1376264 | tf_op jit(solution)/shard_map/ppermute | solution.py:426
  111.3 11.8 %copy-start = (bf16[64,64]{1,0:T(8,128)(2,1)S(1)}, bf16[64,64]{1,0:T(8,128)(2,1)}, u32[]{:S(2)}) copy-start(bf16[64,64]{1,0:T(8,128)(2,1)} %lo_ref.7) | copy-start | bytes 24580
  111.4 11.8 %collective-permute-start.6 = (bf16[128,2,56,128]{3,2,1,0:T(8,128)(2,1)}, bf16[128,2,56,128]{3,2,1,0:T(8,128)(2,1)}, u32[]{:S(2)}, u32[]{:S(2)}) collective-permute-start(bf16[128,2,56,128]{3,2,1,0:T(8,128)(2,1)} %gate.1.own_ref), channel_id=1, source_target_pairs={{0,1},{1,0},{2,3},{3,2},{4,5},{5,4},{6,7},{7,6},{8,9},{9,8},{10,11... | collective-permute-start | bytes 11010056 | tf_op jit(solution)/shard_map/ppermute | solution.py:395
  112.8 58.2 %all-to-all-start = ((bf16[32,4,56,128]{3,2,1,0:T(8,128)(2,1)}), bf16[32,4,56,128]{3,2,1,0:T(8,128)(2,1)S(1)}, u32[]{:S(2)}, u32[]{:S(2)}) async-start(bf16[32,4,56,128]{3,2,1,0:T(8,128)(2,1)} %join.1.refs_1_), calls=%async_computation | async-start | bytes 3670016 | tf_op jit(solution)/shard_map/all_to_all | solution.py:431
  126.8 22.0 %collective-permute-start.8 = (bf16[64,7168]{1,0:T(8,128)(2,1)}, bf16[64,7168]{1,0:T(8,128)(2,1)}, u32[]{:S(2)}, u32[]{:S(2)}) collective-permute-start(bf16[64,7168]{1,0:T(8,128)(2,1)} %both0.2.refs_0_), channel_id=1, source_target_pairs={{0,2},{2,0},{1,3},{3,1},{4,6},{6,4},{5,7},{7,5},{8,10},{10,8},{9,1... | collective-permute-start | bytes 2752520 | tf_op jit(solution)/shard_map/ppermute | solution.py:395
  130.9 37.6 %collective-permute-start.7 = (bf16[64,7168]{1,0:T(8,128)(2,1)}, bf16[64,7168]{1,0:T(8,128)(2,1)}, u32[]{:S(2)}, u32[]{:S(2)}) collective-permute-start(bf16[64,7168]{1,0:T(8,128)(2,1)} %both1.2.refs_0_), channel_id=1, source_target_pairs={{0,2},{2,0},{1,3},{3,1},{4,6},{6,4},{5,7},{7,5},{8,10},{10,8},{9,1... | collective-permute-start | bytes 2752520 | tf_op jit(solution)/shard_map/ppermute | solution.py:395
